TPU v7x, 32 devices: a whole 2x2x4 slice. The times are simulated.
32 devices in a mesh: dp: 4 (over y, x), seq: 8 (over z, core).
Axes of the slice: x: 2, y: 2, z: 4, core: 2. Of those that a mesh axis runs over, the one named last changes fastest.
Arguments:
- inputs: bfloat16 [8, 2048, 512], P('dp', 'seq'), may hold values from -6 to 6
- lengths: int32 [8], P('dp'), may hold values from 1 to 2048, as said below
- ln_gain: float32 [512], P(('dp', 'seq')), may hold values from 0.5 to 1.5
- ln_bias: float32 [512], P(('dp', 'seq')), may hold values from -4 to 4
- lam_log: float32 [512, 64], P(('dp', 'seq'))
- lam_im: float32 [512, 64], P(('dp', 'seq')), may hold values from -3.140625 to 3.140625
- log_dt: float32 [512], P(('dp', 'seq')), may hold values from -0.35 to 0.35
- mix_weight: float32 [512, 128], P(('dp', 'seq'))
- skip: float32 [512], P(('dp', 'seq')), may hold values from -6 to 6
- glu_weight: bfloat16 [512, 1024], P(('dp', 'seq')), may hold values from -0.25 to 0.25
- glu_bias: float32 [1024], P(('dp', 'seq')), may hold values from -4 to 4
- out_grad: bfloat16 [8, 2048, 512], P('dp', 'seq'), may hold values from -6 to 6
Outputs:
- output: bfloat16 [8, 2048, 512], P('dp', 'seq')
- input_grad: bfloat16 [8, 2048, 512], P('dp', 'seq')
- ln_gain_grad: float32 [512], P(('dp', 'seq'))
- ln_bias_grad: float32 [512], P(('dp', 'seq'))
- lam_log_grad: float32 [512, 64], P(('dp', 'seq'))
- lam_im_grad: float32 [512, 64], P(('dp', 'seq'))
- log_dt_grad: float32 [512], P(('dp', 'seq'))
- mix_weight_grad: float32 [512, 128], P(('dp', 'seq'))
- skip_grad: float32 [512], P(('dp', 'seq'))
- glu_weight_grad: float32 [512, 1024], P(('dp', 'seq'))
- glu_bias_grad: float32 [1024], P(('dp', 'seq'))
Inputs may be any that keep to these rules, and one draw needn't show every extreme that they name: `lengths`: in each block of 2 consecutive sequences (those of one index of dp) one sequence has length 2048.
All inputs are finite; a program needn't handle non-finite values.
Results may differ from a plain program's by a relative error of at most 0.0056.
Values may be sent and summed in bfloat16 or wider, within the bound.
A program may use at most 320 MiB of HBM per device.

v0:
```python
import math
from functools import partial

import jax
import jax.numpy as jnp
from jax import lax
from jax.experimental import pallas as pl
from jax.experimental.pallas import tpu as pltpu
from jax.sharding import PartitionSpec as P

BLOCK = 128
EPS = 1e-05
HIGH = lax.Precision.HIGHEST
BOTH = ("dp", "seq")


def halves(packed):
    count = packed.shape[-1] // 2
    return (packed[..., :count], packed[..., count:])


def cmul(first, second):
    first_re, first_im = halves(first)
    second_re, second_im = halves(second)
    return jnp.concatenate(
        [first_re * second_re - first_im * second_im, first_re * second_im + first_im * second_re],
        axis=-1,
    )


def conjugate(packed):
    real_half, imag_half = halves(packed)
    return jnp.concatenate([real_half, -imag_half], axis=-1)


def coefficients(lam_log, lam_im, log_dt, mix_weight):
    spacing = jnp.exp(log_dt)[:, None]
    rate = jnp.exp(lam_log)
    shrink = -rate * spacing
    angle = lam_im * spacing
    scale = jnp.exp(shrink)
    decay = jnp.concatenate([scale * jnp.cos(angle), scale * jnp.sin(angle)], axis=-1)
    less_re = jnp.expm1(shrink) * jnp.cos(angle) - 2.0 * jnp.sin(0.5 * angle) ** 2
    less_im = scale * jnp.sin(angle)
    modulus = rate * rate + lam_im * lam_im
    ratio = jnp.concatenate(
        [
            (lam_im * less_im - rate * less_re) / modulus,
            -(rate * less_im + lam_im * less_re) / modulus,
        ],
        axis=-1,
    )
    return (decay, cmul(mix_weight, ratio))


def powers(decay):
    real_half, imag_half = halves(decay)
    table = jnp.concatenate([jnp.ones_like(real_half), jnp.zeros_like(imag_half)], axis=-1)[:, None]
    step = decay[:, None]
    while table.shape[1] < BLOCK:
        table = jnp.concatenate([table, cmul(step, table)], axis=1)
        step = cmul(step, step)
    return (table, step[:, 0])


def link(earlier, later):
    return (cmul(earlier[0], later[0]), cmul(later[0], earlier[1]) + later[1])


def shifted(pieces, step, back):
    leads = jnp.broadcast_to(step[:, None, None], pieces.shape)
    _, reach = lax.associative_scan(link, (leads, pieces), axis=2, reverse=back)
    none = jnp.zeros_like(reach[:, :, :1])
    if back:
        return jnp.concatenate([reach[:, :, 1:], none], axis=2)
    return jnp.concatenate([none, reach[:, :, :-1]], axis=2)


def to_owner(rows):
    count, span, width = rows.shape
    groups, parts = (lax.axis_size("dp"), lax.axis_size("seq"))
    own = width // (groups * parts)
    sent = rows.reshape(count * span, width).T.reshape(-1, own, count, span)
    held = lax.all_to_all(sent, BOTH, 0, 0, tiled=True).reshape(groups, parts, own, count, span)
    held = held.transpose(2, 0, 3, 1, 4).reshape(own, groups * count, -1, BLOCK)
    return held


def to_holder(held, count, span):
    groups, parts = (lax.axis_size("dp"), lax.axis_size("seq"))
    own = held.shape[0]
    sent = held.astype(jnp.bfloat16).reshape(own, groups, count, parts, span).transpose(1, 3, 0, 2, 4)
    sent = sent.reshape(groups * parts, own, count, span)
    rows = lax.all_to_all(sent, BOTH, 0, 0, tiled=True)
    return rows.reshape(-1, count * span).T.reshape(count, span, -1).astype(jnp.float32)


def per_device(
    inputs,
    lengths,
    ln_gain,
    ln_bias,
    lam_log,
    lam_im,
    log_dt,
    mix_weight,
    skip,
    glu_weight,
    glu_bias,
    out_grad,
):
    count, span, width = inputs.shape
    offset = lax.axis_index("seq") * span
    positions = offset + jnp.arange(span, dtype=jnp.int32)
    valid = (positions[None, :] < lengths[:, None]).astype(jnp.float32)[..., None]
    rows = lax.all_gather(glu_weight, BOTH, axis=0, tiled=True)
    shift = lax.all_gather(glu_bias, BOTH, axis=0, tiled=True)
    spans = lax.all_gather(lengths, "dp", axis=0, tiled=True)
    whole_span = span * lax.axis_size("seq")
    mask = (jnp.arange(whole_span, dtype=jnp.int32)[None] < spans[:, None]).astype(jnp.float32)
    mask = mask.reshape(1, -1, whole_span // BLOCK, BLOCK)

    tokens = inputs.astype(jnp.float32)
    mean = jnp.mean(tokens, axis=-1, keepdims=True)
    centered = tokens - mean
    inverse = lax.rsqrt(jnp.mean(centered * centered, axis=-1, keepdims=True) + EPS)
    normed = centered * inverse

    (decay, coeff), coeff_pull = jax.vjp(coefficients, lam_log, lam_im, log_dt, mix_weight)
    base, whole = powers(decay)
    down = base[:, ::-1]
    real_half, imag_half = halves(coeff)
    kernel = jnp.einsum("cz,ckz->ck", conjugate(coeff), base, precision=HIGH)
    lead = cmul(coeff, decay)[:, None]
    up = conjugate(cmul(lead, base))
    back = conjugate(cmul(lead, down))
    steps = jnp.arange(BLOCK)
    lag = steps[:, None] - steps[None, :]
    toeplitz = jnp.where(lag >= 0, kernel[:, jnp.maximum(lag, 0)], 0.0)
    ramp = steps.astype(jnp.float32)[:, None]

    gain, bias, skipping = (p[:, None, None, None] for p in (ln_gain, ln_bias, skip))
    own_normed = to_owner(normed)
    drive = (own_normed * gain + bias) * mask
    entering = shifted(jnp.einsum("cbqj,cjz->cbqz", drive, down, precision=HIGH), whole, False)
    response = jnp.einsum("cij,cbqj->cbqi", toeplitz, drive, precision=HIGH)
    response += jnp.einsum("ciz,cbqz->cbqi", up, entering, precision=HIGH) + skipping * drive
    activated, gelu_pull = jax.vjp(partial(jax.nn.gelu, approximate=False), response)
    activated = to_holder(activated, count, span).astype(jnp.bfloat16).reshape(-1, width)
    pre = jnp.dot(activated, rows, preferred_element_type=jnp.float32) + shift
    gate = jax.nn.sigmoid(pre[:, width:])
    flat_valid = valid.reshape(-1, 1)
    result = (tokens + (pre[:, :width] * gate * flat_valid).reshape(tokens.shape)).astype(jnp.bfloat16)
    upstream = out_grad.astype(jnp.float32)
    gated = upstream.reshape(-1, width) * flat_valid
    pre_grad = jnp.concatenate(
        [gated * gate, gated * pre[:, :width] * gate * (1.0 - gate)], axis=-1
    ).astype(jnp.bfloat16)
    rows_grad = lax.dot_general(
        activated, pre_grad, (((0,), (0,)), ((), ())), preferred_element_type=jnp.float32
    )
    shift_grad = jnp.sum(pre_grad.astype(jnp.float32), axis=0)
    act_grad = lax.dot_general(
        pre_grad, rows, (((1,), (1,)), ((), ())), preferred_element_type=jnp.float32
    )
    response_grad = gelu_pull(to_owner(act_grad.reshape(tokens.shape)))[0]

    skip_grad = jnp.sum(response_grad * drive, axis=(1, 2, 3))
    outflow = jnp.einsum("cbqt,ctz->cbqz", response_grad, base, precision=HIGH)
    leaving = shifted(outflow, whole, True)
    drive_grad = jnp.einsum("cij,cbqi->cbqj", toeplitz, response_grad, precision=HIGH)
    drive_grad += jnp.einsum("cjz,cbqz->cbqj", back, leaving, precision=HIGH) + skipping * response_grad
    norm_grad = drive_grad * mask
    gain_grad = jnp.sum(norm_grad * own_normed, axis=(1, 2, 3))
    bias_grad = jnp.sum(norm_grad, axis=(1, 2, 3))
    scaled = to_holder(norm_grad * gain, count, span)
    token_grad = upstream + inverse * (
        scaled
        - jnp.mean(scaled, axis=-1, keepdims=True)
        - normed * jnp.mean(scaled * normed, axis=-1, keepdims=True)
    )

    cross = jnp.einsum("cbqj,cbqi->cij", drive, response_grad, precision=HIGH)
    lags = jnp.stack([jnp.trace(cross, offset=-k, axis1=1, axis2=2) for k in range(BLOCK)], axis=-1)
    second = jnp.einsum("cbqj,cjz->cbqz", drive, down * ramp[::-1], precision=HIGH)
    third = jnp.einsum("cbqt,ctz->cbqz", response_grad, base * (ramp + 1.0), precision=HIGH)
    total = partial(jnp.sum, axis=(1, 2))
    moment = cmul(decay, total(cmul(entering, outflow))) + jnp.einsum("ck,ckz->cz", lags, base, precision=HIGH)
    before = jnp.concatenate([jnp.zeros_like(base[:, :1]), base[:, :-1]], axis=1) * ramp
    paired = BLOCK * cmul(whole, total(cmul(leaving, entering)))
    paired += total(cmul(leaving, second) + cmul(entering, third))
    paired = cmul(coeff, paired + jnp.einsum("ck,ckz->cz", lags, before, precision=HIGH))
    rate_grad, turn_grad, spacing_grad, mixing_grad = coeff_pull((conjugate(paired), conjugate(moment)))

    scatter = partial(lax.psum_scatter, axis_name=BOTH, scatter_dimension=0, tiled=True)
    return (
        result,
        token_grad.astype(jnp.bfloat16),
        gain_grad,
        bias_grad,
        rate_grad,
        turn_grad,
        spacing_grad,
        mixing_grad,
        skip_grad,
        scatter(rows_grad),
        scatter(shift_grad),
    )


MESH = pl.DeviceIdType.MESH
F32, BF16, I16 = (jnp.float32, jnp.bfloat16, jnp.int16)
STEPS = 32700.0
GROUP = 4
HALVES = 2


def two(value):
    high = value.astype(BF16)
    return (high, (value - high.astype(F32)).astype(BF16))


def dot(left, right, dims=((1,), (0,))):
    return lax.dot_general(left, right, (dims, ((), ())), preferred_element_type=F32)


TURNED = ((1,), (1,))
SIDEWAYS = ((0,), (0,))


def product(left, table, dims=((1,), (0,))):
    return dot(left[0], table[0], dims) + dot(left[1], table[0], dims) + dot(left[0], table[1], dims)


def times(value, factor):
    return (value[0] * factor[0] - value[1] * factor[1], value[0] * factor[1] + value[1] * factor[0])


def plus(first, second):
    return (first[0] + second[0], first[1] + second[1])


def choose(condition, first, second):
    return (jnp.where(condition, first[0], second[0]), jnp.where(condition, first[1], second[1]))


def split(value):
    return (value[:, :BLOCK], value[:, BLOCK:])


def beside(*parts):
    return jnp.concatenate(parts, axis=1)


def over(*parts):
    return jnp.concatenate(parts, axis=0)


def total_rows(value):
    return jnp.sum(value, axis=0, keepdims=True)


def small_expm1(value):
    near = jnp.abs(value) < 0.5
    small = jnp.where(near, value, 0.0)
    series = jnp.ones_like(small)
    for order in range(10, 1, -1):
        series = 1.0 + small * (1.0 / order) * series
    return jnp.where(near, small * series, jnp.exp(value) - 1.0)


def coefficient_parts(lam_log, lam_im, log_dt, mix_re, mix_im):
    spacing, rate = (jnp.exp(log_dt), jnp.exp(lam_log))
    shrink, angle = (-rate * spacing, lam_im * spacing)
    scale = jnp.exp(shrink)
    cosine, sine, half = (jnp.cos(angle), jnp.sin(angle), jnp.sin(0.5 * angle))
    less_re = small_expm1(shrink) * cosine - 2.0 * half * half
    less_im = scale * sine
    modulus = rate * rate + lam_im * lam_im
    ratio = (
        (lam_im * less_im - rate * less_re) / modulus,
        -(rate * less_im + lam_im * less_re) / modulus,
    )
    return (scale * cosine, less_im) + times((mix_re, mix_im), ratio)


def whole_kernel(
    size,
    inputs, lengths, ln_gain, ln_bias, lam_log, lam_im, log_dt, mix_weight, skip, glu_weight, glu_bias, out_grad,
    result, token_grad, gain_grad, bias_grad, rate_grad, turn_grad, spacing_grad, mixing_grad, skip_grad,
    rows_grad, shift_grad,
    s,
):
    groups, parts, own, width, span, count = size
    local, blocks, zs = (parts // HALVES, span // BLOCK, parts // 2)
    members = groups * local
    tiles, couples, states = (width // BLOCK, own // 2, lam_log.shape[1])
    wide = 2 * width
    dp, seq = (lax.axis_index("dp"), lax.axis_index("seq"))
    core, z = (lax.rem(seq, 2), seq // 2)
    half, here = (seq // local, lax.rem(seq, local))
    other = 1 - half
    me = dp * local + here
    partner = (dp, other * local + here)

    def place(member):
        return (member // local, half * local + lax.rem(member, local))

    def send(source, target, sems, device):
        pltpu.make_async_remote_copy(
            src_ref=source, dst_ref=target, send_sem=sems.at[0], recv_sem=sems.at[1],
            device_id=device, device_id_type=MESH,
        ).start()

    def wait_for(ref, sem):
        pltpu.make_async_copy(ref, ref, sem).wait()

    def to_owners(out, into, sems):
        def one(k, carry):
            member = lax.rem(me + k, members)
            send(out.at[member // local, lax.rem(member, local)], into.at[me], sems, place(member))
            return carry

        lax.fori_loop(1, members, one, 0)

    def to_holders(out, into, sems):
        def one(k, carry):
            member = lax.rem(me + k, members)
            send(out.at[member], into.at[dp, here], sems, place(member))
            return carry

        lax.fori_loop(1, members, one, 0)

    def to_all(out, into, sems):
        def one(k, carry):
            send(out, into.at[me], sems, place(lax.rem(me + k, members)))
            return carry

        lax.fori_loop(1, members, one, 0)

    def many(ref):
        return ref.at[pl.ds(0, members - 1)]

    barrier = pltpu.get_barrier_semaphore()

    def greet(k, carry):
        member = place(lax.rem(me + k, members))
        pl.semaphore_signal(barrier, inc=1, device_id=member, device_id_type=MESH)
        return carry

    lax.fori_loop(1, members, greet, 0)
    for k in range(zs // HALVES):
        there = other * local + 2 * k + core
        pl.semaphore_signal(barrier, inc=1, device_id=(dp, there), device_id_type=MESH)

    lane = lax.broadcasted_iota(jnp.int32, (1, span), 1) + seq * span
    quantum = math.sqrt(width) / STEPS

    def chunk_rows(j):
        per = BLOCK // own
        for i in range(per):
            shard = j * per + i
            yield slice(i * own, (i + 1) * own), shard // parts, shard % parts // local, shard % local

    def norm(m):
        tokens = inputs[m].T
        s.tokens[m] = tokens
        total = jnp.zeros((1, span), F32)
        for j in range(tiles):
            total += total_rows(tokens[j * BLOCK : (j + 1) * BLOCK].astype(F32))
        mean = total * (1.0 / width)
        total = jnp.zeros((1, span), F32)
        for j in range(tiles):
            off = tokens[j * BLOCK : (j + 1) * BLOCK].astype(F32) - mean
            total += total_rows(off * off)
        inverse = lax.rsqrt(total * (1.0 / width) + EPS)
        valid = (lane < lengths[m]).astype(F32)
        s.inverse[m : m + 1] = inverse
        s.valid[m : m + 1] = valid
        for j in range(tiles):
            normed = (tokens[j * BLOCK : (j + 1) * BLOCK].astype(F32) - mean) * inverse
            s.normed[m, j * BLOCK : (j + 1) * BLOCK] = normed
            coded = jnp.round(normed * valid * (1.0 / quantum)).astype(I16)
            for rows, a, k, p in chunk_rows(j):
                s.x_out[k, m, a, p] = coded[rows]
        for k in range(HALVES):
            s.x_in[k, m, pl.ds(me, 1)] = s.x_out[k, m, dp, pl.ds(here, 1)]

    for m in range(count):
        norm(m)

    row_lane = lax.broadcasted_iota(jnp.int32, (1, BLOCK), 1)
    row = jnp.zeros((1, BLOCK), F32)
    for m in range(count):
        row = jnp.where(row_lane == m, lengths[m].astype(F32), row)
    s.note_out[0] = row
    s.note_in[pl.ds(me, 1)] = row[None]

    own_row = lax.broadcasted_iota(jnp.int32, (own, BLOCK), 0)
    own_lane = lax.broadcasted_iota(jnp.int32, (own, BLOCK), 1)
    scalars = jnp.zeros((own, BLOCK), F32)
    shifts = jnp.zeros((own, BLOCK), F32)
    for c in range(own):
        for i, ref in enumerate((log_dt, ln_gain, ln_bias, skip)):
            scalars = jnp.where((own_row == c) & (own_lane == i), ref[c], scalars)
        for i in range(2):
            shifts = jnp.where((own_row == c) & (own_lane % 2 == i), glu_bias[i * own + c], shifts)
    s.params[pl.ds(half, 1), :, :states] = lam_log[...][None]
    s.params[pl.ds(half, 1), :, states : 2 * states] = lam_im[...][None]
    s.params[pl.ds(half, 1), :, BLOCK : 2 * BLOCK] = mix_weight[...][None]
    s.params[pl.ds(half, 1), :, 2 * BLOCK :] = scalars[None]
    high = shifts.astype(BF16)
    rest = shifts - high.astype(F32)
    middle = rest.astype(BF16)
    lowest = (rest - middle.astype(F32)).astype(BF16)
    thirds = jnp.where(own_lane < 2, high, jnp.where(own_lane < 4, middle, lowest))
    s.weight_out[:, :wide] = glu_weight[...]
    s.weight_out[:, wide:] = thirds
    s.weight[pl.ds(dp, 1), pl.ds(z, 1), pl.ds(core, 1)] = s.weight_out[...][None, None, None]

    def weight_hop(hop):
        sems = s.weight_sem.at[hop]
        if hop == 0:
            for k in range(1, zs):
                there = lax.rem(z + k, zs)
                send(s.weight_out, s.weight.at[dp, z, core], sems, (dp, there * 2 + core))
        elif hop == 1:
            for k in range(1, groups):
                mine = s.weight.at[dp, :, core]
                send(mine, mine, sems, (lax.rem(dp + k, groups), seq))
        else:
            mine = s.weight.at[:, :, core]
            send(mine, mine, sems, (dp, z * 2 + 1 - core))

    def weight_wait(hop):
        if hop == 0:
            ref = s.weight.at[0, pl.ds(0, zs - 1), 0]
        elif hop == 1:
            ref = s.weight.at[pl.ds(0, groups - 1), :, 0]
        else:
            ref = s.weight.at[:, :, 0]
        wait_for(ref, s.weight_sem.at[hop, 0])
        wait_for(ref, s.weight_sem.at[hop, 1])

    pl.semaphore_wait(barrier, members - 1 + zs // HALVES)
    send(s.params.at[half], s.params.at[half], s.params_sem, partner)
    to_all(s.note_out.at[0], s.note_in, s.note_sem)
    for k in range(HALVES):
        for m in range(count):
            to_owners(s.x_out.at[k, m], s.x_in.at[k, m], s.x_sem.at[k, m])
    weight_hop(0)

    wait_for(s.params.at[0], s.params_sem.at[0])
    wait_for(s.params.at[0], s.params_sem.at[1])
    pair_low = lax.broadcasted_iota(jnp.int32, (couples, BLOCK), 1) < states

    def coupled(value):
        s.turn[...] = value
        even = s.turn[pl.ds(0, couples, stride=2), :]
        odd = s.turn[pl.ds(1, couples, stride=2), :]
        return jnp.where(pair_low, even, pltpu.roll(odd, states, 1))

    def raw_params(k):
        packed = [s.params[k, :, i * BLOCK : (i + 1) * BLOCK] for i in range(3)]
        lam, mix, rest = packed
        log_step = jnp.broadcast_to(rest[:, :1], (own, BLOCK))
        return tuple(
            coupled(value)
            for value in (lam, pltpu.roll(lam, states, 1), log_step, mix, pltpu.roll(mix, states, 1))
        )

    for k in range(HALVES):
        rest = s.params[k, :, 2 * BLOCK :]
        for i in range(1, 4):
            s.scalars[i - 1, k * own : (k + 1) * own] = jnp.broadcast_to(rest[:, i : i + 1], (own, BLOCK))
        parts_k = coefficient_parts(*raw_params(k))
        rows = slice(k * couples, (k + 1) * couples)
        decay, coeff = (parts_k[:2], parts_k[2:])
        s.coeff[0, rows], s.coeff[1, rows] = coeff
        s.lead[0, rows], s.lead[1, rows] = times(coeff, decay)
        power = decay
        for bit in range(s.power.shape[0]):
            s.power[bit, 0, rows], s.power[bit, 1, rows] = power
            power = times(power, power)

    def power_of(bit, p):
        return (s.power[bit, 0, pl.ds(p, 1), :], s.power[bit, 1, pl.ds(p, 1), :])

    square = (BLOCK, BLOCK)
    row_id = lax.broadcasted_iota(jnp.int32, square, 0)
    lane_id = lax.broadcasted_iota(jnp.int32, square, 1)
    ramp = row_id.astype(F32)
    first_states = lax.rem(lax.broadcasted_iota(jnp.int32, (BLOCK, 2 * BLOCK), 1), BLOCK) < states

    def stacked(value):
        none = jnp.zeros_like(value)
        return over(jnp.where(first_states, value, none), jnp.where(first_states, none, value))

    def put_table(ref, p, value):
        for i, part in enumerate(two(beside(*value))):
            ref[p, i] = stacked(part)

    def tables(p):
        eight = row_id[:8]
        unit = (jnp.ones((8, BLOCK), F32), jnp.zeros((8, BLOCK), F32))
        base, down = (unit, unit)
        for bit in range(3):
            step = power_of(bit, p)
            base = choose((eight >> bit) & 1 == 1, times(base, step), base)
            down = choose(((7 - eight) >> bit) & 1 == 1, times(down, step), down)
        for bit in range(3, 7):
            step = power_of(bit, p)
            more, most = (times(base, step), times(down, step))
            base = (over(base[0], more[0]), over(base[1], more[1]))
            down = (over(most[0], down[0]), over(most[1], down[1]))
        lead = (s.lead[0, pl.ds(p, 1), :], s.lead[1, pl.ds(p, 1), :])
        up, back = (times(base, lead), times(down, lead))
        put_table(s.base, p, base)
        put_table(s.down, p, down)
        put_table(s.up, p, (up[0], -up[1]))
        put_table(s.back, p, (back[0], -back[1]))
        for ref, value, slope in (
            (s.base_ramp, base, ramp + 1.0),
            (s.down_ramp, down, BLOCK - 1.0 - ramp),
        ):
            ref[p] = stacked(beside(value[0] * slope, value[1] * slope).astype(BF16))
        weights = beside(s.coeff[0, pl.ds(p, 1), :], -s.coeff[1, pl.ds(p, 1), :])
        weights = jnp.broadcast_to(weights, (8, 2 * BLOCK))
        pick = lax.rem(lax.broadcasted_iota(jnp.int32, (8, 2 * BLOCK), 1), BLOCK) < states
        pick = pick == (lax.broadcasted_iota(jnp.int32, (8, 2 * BLOCK), 0) == 0)
        kernel = lax.dot_general(
            jnp.where(pick, weights, 0.0), beside(*base), (TURNED, ((), ())),
            preferred_element_type=F32, precision=HIGH,
        )
        for i in range(2):
            slanted = jnp.broadcast_to(kernel[i : i + 1], square)
            slanted = pltpu.roll(slanted, 0, 1, stride=1, stride_axis=0)
            side = slice(i * BLOCK, (i + 1) * BLOCK)
            off = slice((1 - i) * BLOCK, (2 - i) * BLOCK)
            for part, value in enumerate(two(jnp.where(lane_id >= row_id, slanted, 0.0))):
                s.toeplitz[p, part, side, side] = value
                s.toeplitz[p, part, side, off] = jnp.zeros(square, BF16)

    def over_couples(k, body, group=GROUP):
        def some(g, carry):
            for u in range(group):
                body(k * couples + g * group + u, g * group + u)
            return carry

        lax.fori_loop(0, couples // group, some, 0)

    for k in range(HALVES):
        over_couples(k, lambda p, c: tables(p), 2)

    half_rows = count * members
    full_rows = blocks * half_rows
    place_of = lax.rem(lax.broadcasted_iota(jnp.int32, (half_rows, BLOCK), 0), local)
    place_lane = lax.broadcasted_iota(jnp.int32, (half_rows, BLOCK), 1)
    step_bit = 7 + blocks.bit_length() - 1

    def rows_in(ref, k):
        for m in range(count):
            for q in range(blocks):
                piece = ref[k, m, :, :, q * BLOCK : (q + 1) * BLOCK]
                s.stage_in[q, m] = piece.astype(F32).reshape(members * own, BLOCK)

    def rows_out(ref, k):
        for m in range(count):
            for q in range(blocks):
                ref[k, m, :, :, q * BLOCK : (q + 1) * BLOCK] = (
                    s.stage_out[q, m].astype(BF16).reshape(members, own, BLOCK)
                )

    def gather_couple(c):
        sides = []
        for i in range(2):
            sides.append(
                over(
                    *(
                        s.stage_in[q, m, pl.ds(2 * c + i, members, stride=own), :]
                        for q in range(blocks)
                        for m in range(count)
                    )
                )
            )
        return beside(*sides)

    def put_couple(c, value):
        for i, side in enumerate(split(value)):
            for q in range(blocks):
                for m in range(count):
                    first = (q * count + m) * members
                    s.stage_out[q, m, pl.ds(2 * c + i, members, stride=own), :] = side[first : first + members]

    def scalar_rows(i, p):
        return beside(s.scalars[i, pl.ds(2 * p, 1), :], s.scalars[i, pl.ds(2 * p + 1, 1), :])

    def by_block(value):
        return [split(value[q * half_rows : (q + 1) * half_rows]) for q in range(blocks)]

    def scan(flows, p, upward):
        block_step = power_of(7, p)
        flows = flows if upward else flows[::-1]
        total = flows[0]
        for flow in flows[1:]:
            total = plus(times(total, block_step), flow)

        def moved(value, reach):
            shift = reach if upward else half_rows - reach
            inside = place_of >= reach if upward else place_of < local - reach
            return tuple(jnp.where(inside, pltpu.roll(part, shift, 0), 0.0) for part in value)

        reach = 1
        while reach < local:
            total = plus(total, times(moved(total, reach), power_of(step_bit + reach.bit_length() - 1, p)))
            reach *= 2
        return moved(total, 1), total

    def carried(state, ref, p, upward):
        for j in range(local):
            for i in range(2):
                s.widen[p, i, pl.ds(j, count * groups, stride=local), :] = ref[p, i]
        carry = (s.widen[p, 0], s.widen[p, 1])
        distance = place_of if upward else local - 1 - place_of
        for bit in range(local.bit_length() - 1):
            further = times(carry, power_of(step_bit + bit, p))
            carry = choose((distance >> bit) & 1 == 1, further, carry)
        return plus(state, carry)

    def through(state, flows, p, upward):
        block_step = power_of(7, p)
        listing = [state]
        flows = flows if upward else flows[::-1]
        for flow in flows[:-1]:
            state = plus(times(state, block_step), flow)
            listing.append(state)
        listing = listing if upward else listing[::-1]
        return over(*(beside(*state) for state in listing))

    def read_notes():
        wait_for(many(s.note_in), s.note_sem.at[1])
        notes = s.note_in[...].reshape(members, BLOCK)
        member_lane = lax.broadcasted_iota(jnp.int32, (members, BLOCK), 1)
        member_place = lax.rem(lax.broadcasted_iota(jnp.int32, (members, BLOCK), 0), local)
        start = (half * local + member_place) * span + member_lane
        for m in range(count):
            length = jnp.sum(jnp.where(member_lane == m, notes, 0.0), axis=1, keepdims=True)
            for q in range(blocks):
                first = (q * count + m) * members
                within = ((start + q * BLOCK).astype(F32) < length).astype(F32)
                s.mask[first : first + members] = beside(within, within)

    def pick_last(p, total, out, first):
        for i in range(2):
            s.widen[p, i] = total[i]
            out[p, i] = s.widen[p, i, pl.ds(first, count * groups, stride=local), :]

    def forward_first(k):
        for m in range(count):
            wait_for(many(s.x_in.at[k, m]), s.x_sem.at[k, m, 1])
        rows_in(s.x_in, k)

        def inflow(p, c):
            own_normed = gather_couple(c) * quantum
            drive = (own_normed * scalar_rows(0, p) + scalar_rows(1, p)) * s.mask[...]
            s.own_normed[p] = own_normed
            s.drive[p] = drive
            s.inflow[p] = product(two(drive), s.down[p])

        over_couples(k, inflow)

        def scanned(p, c):
            state, total = scan(by_block(s.inflow[p]), p, True)
            s.entering[p, :half_rows] = beside(*state)
            pick_last(p, total, s.carry_out, local - 1)

        over_couples(k, scanned)
        rows = pl.ds(k * couples, couples)

        @pl.when(half == 0)
        def _():
            send(s.carry_out.at[rows], s.carry_in.at[rows], s.carry_sem.at[k], partner)

    def forward_second(k):
        rows = pl.ds(k * couples, couples)

        @pl.when(half == 0)
        def _():
            s.carry_in[rows] = jnp.zeros((couples, 2, count * groups, BLOCK), F32)

        @pl.when(half == 1)
        def _():
            wait_for(s.carry_in.at[rows], s.carry_sem.at[k, 1])

        def complete(p, c):
            state = carried(split(s.entering[p, :half_rows]), s.carry_in, p, True)
            s.entering[p] = through(state, by_block(s.inflow[p]), p, True)

        over_couples(k, complete)

        def respond(p, c):
            drive = s.drive[p]
            response = product(two(drive), s.toeplitz[p])
            response += product(two(s.entering[p]), s.up[p], TURNED)
            response += scalar_rows(2, p) * drive
            share_below = 0.5 * (1.0 + lax.erf(response * math.sqrt(0.5)))
            density = jnp.exp(-0.5 * response * response) * (1.0 / math.sqrt(2.0 * math.pi))
            s.slope[p] = share_below + response * density
            put_couple(c, response * share_below)

        over_couples(k, respond)
        rows_out(s.a_out, k)
        for m in range(count):
            s.a_in[m, dp, k, pl.ds(here, 1)] = s.a_out[k, m, pl.ds(me, 1)]
            to_holders(s.a_out.at[k, m], s.a_in.at[m, :, k], s.a_sem.at[k, m])

    read_notes()
    for k in range(HALVES):
        forward_first(k)
        if k == 0:
            weight_wait(0)
            weight_hop(1)
    for k in range(HALVES):
        forward_second(k)
        if k == 0:
            weight_wait(1)
            weight_hop(2)

    for m in range(count):
        s.upstream[m] = out_grad[m].T
    weight_wait(2)
    for j in range(tiles):
        rows = slice(j * BLOCK, (j + 1) * BLOCK)
        per = BLOCK // own
        flat = s.weight[...].reshape(-1, own, wide + BLOCK)[j * per : (j + 1) * per].reshape(BLOCK, -1)
        s.flat[rows] = flat[:, :wide]
        s.flipped[:, rows] = flat[:, :wide].T
        shifts = flat[:, wide:].astype(F32)
        shifts = shifts + pltpu.roll(shifts, BLOCK - 2, 1) + pltpu.roll(shifts, BLOCK - 4, 1)
        for i in range(2):
            column = jnp.broadcast_to(shifts[:, i : i + 1], (BLOCK, BLOCK)).reshape(per, own, BLOCK)
            for n in range(per):
                first = ((j * per + n) * 2 + i) * own
                s.shift[first : first + own] = column[n]

    def project(m):
        for k in range(HALVES):
            ref = s.a_out.at[k, m, pl.ds(0, members - 1)]
            wait_for(ref, s.a_sem.at[k, m, 1])
        activated = s.a_in[m].reshape(width, span)
        valid = s.valid[m : m + 1]
        for j in range(tiles):
            rows = slice(j * BLOCK, (j + 1) * BLOCK)
            gates = slice(width + j * BLOCK, width + (j + 1) * BLOCK)
            value = dot(s.flipped[rows], activated) + beside(*[s.shift[rows]] * blocks)
            gate = jax.nn.sigmoid(dot(s.flipped[gates], activated) + beside(*[s.shift[gates]] * blocks))
            gated = s.upstream[m, rows].astype(F32) * valid
            s.pre_grad[rows] = (gated * gate).astype(BF16)
            s.pre_grad[gates] = (gated * value * gate * (1.0 - gate)).astype(BF16)
            s.result[m, rows] = (s.tokens[m, rows].astype(F32) + value * gate * valid).astype(BF16)
        largest = jnp.zeros((1, 1), F32)
        for j in range(tiles):
            rows = slice(j * BLOCK, (j + 1) * BLOCK)
            piece = dot(s.flat[rows], s.pre_grad[...])
            s.act_grad[rows] = piece
            largest = jnp.maximum(largest, jnp.max(jnp.abs(piece), axis=(0, 1), keepdims=True))
        largest = jnp.maximum(largest, 1e-30)
        s.scale_out[m] = jnp.broadcast_to(largest * (1.0 / STEPS), (1, BLOCK))
        s.scale_in[m, pl.ds(me, 1)] = s.scale_out[m][None]
        to_all(s.scale_out.at[m], s.scale_in.at[m], s.scale_sem.at[m])
        factor = STEPS / largest
        for j in range(tiles):
            coded = jnp.round(s.act_grad[j * BLOCK : (j + 1) * BLOCK] * factor).astype(I16)
            for rows, a, k, p in chunk_rows(j):
                s.g_out[k, m, a, p] = coded[rows]
        for k in range(HALVES):
            s.g_in[k, m, pl.ds(me, 1)] = s.g_out[k, m, dp, pl.ds(here, 1)]
            to_owners(s.g_out.at[k, m], s.g_in.at[k, m], s.g_sem.at[k, m])
        ones = jnp.ones((span, BLOCK), BF16)
        for j in range(groups):
            per = width // groups
            rows = slice(j * per, (j + 1) * per)
            piece = dot(activated[rows], s.pre_grad[...], TURNED).reshape(zs, 2, own, wide)
            sums = dot(s.pre_grad[2 * j * per : 2 * (j + 1) * per], ones).reshape(zs, 2, 2, own, BLOCK)
            lane4 = lax.broadcasted_iota(jnp.int32, (zs, 2, own, BLOCK), 3)
            sums = jnp.where(lane4 == 0, sums[:, :, 0], jnp.where(lane4 == 1, sums[:, :, 1], 0.0))
            if m == 0:
                s.total[j, :, :, :, :wide] = piece
                s.total[j, :, :, :, wide:] = sums
            else:
                s.total[j, :, :, :, :wide] += piece
                s.total[j, :, :, :, wide:] += sums

    for m in range(count):
        project(m)

    def sum_hop(hop):
        sems = s.sum_sem
        if hop == 0:
            send(s.total.at[:, :, 1 - core], s.sum_core, sems.at[0], (dp, z * 2 + 1 - core))
        elif hop == 1:
            wait_for(s.sum_core, sems.at[0, 0])
            wait_for(s.sum_core, sems.at[0, 1])
            for j in range(groups):
                part = s.total[j, :, pl.ds(core, 1)].reshape(zs, own, -1) + s.sum_core[j]
                s.sum_core[j] = part
                s.sum_dp_out[j] = part.astype(BF16)
            for k in range(1, groups):
                there = lax.rem(dp + k, groups)
                send(s.sum_dp_out.at[there], s.sum_dp_in.at[dp], sems.at[1], (there, seq))
        elif hop == 2:
            ref = s.sum_dp_in.at[pl.ds(0, groups - 1)]
            wait_for(ref, sems.at[1, 0])
            wait_for(ref, sems.at[1, 1])
            part = s.sum_core[dp]
            for k in range(1, groups):
                part += s.sum_dp_in[lax.rem(dp + k, groups)].astype(F32)
            s.sum_core[0] = part
            s.sum_z_out[...] = part.astype(BF16)
            for k in range(1, zs):
                there = lax.rem(z + k, zs)
                send(s.sum_z_out.at[there], s.sum_z_in.at[z], sems.at[2], (dp, there * 2 + core))
        else:
            ref = s.sum_z_in.at[pl.ds(0, zs - 1)]
            wait_for(ref, sems.at[2, 0])
            wait_for(ref, sems.at[2, 1])
            part = s.sum_core[0, pl.ds(z, 1)].reshape(own, -1)
            for k in range(1, zs):
                part += s.sum_z_in[lax.rem(z + k, zs)].astype(F32)
            rows_grad[...] = part[:, :wide]
            columns = part[:, wide:].T
            shift_grad[...] = beside(columns[:1], columns[1:2])

    sum_hop(0)

    def backward_first(k):
        for m in range(count):
            wait_for(many(s.g_in.at[k, m]), s.g_sem.at[k, m, 1])
            if k == 0:
                wait_for(many(s.scale_in.at[m]), s.scale_sem.at[m, 1])
                scale = s.scale_in[m].reshape(members, BLOCK)
                for q in range(blocks):
                    first = (q * count + m) * members
                    s.scales[first : first + members] = beside(scale, scale)
        rows_in(s.g_in, k)

        def outflow(p, c):
            grad = gather_couple(c) * s.scales[...] * s.slope[p]
            s.grad[p] = grad
            s.outflow[p] = product(two(grad), s.base[p])

        over_couples(k, outflow)

        def scanned(p, c):
            state, total = scan(by_block(s.outflow[p]), p, False)
            s.leaving[p, full_rows - half_rows :] = beside(*state)
            pick_last(p, total, s.back_out, 0)

        over_couples(k, scanned)
        rows = pl.ds(k * couples, couples)

        @pl.when(half == 1)
        def _():
            send(s.back_out.at[rows], s.back_in.at[rows], s.back_sem.at[k], partner)

    def backward_second(k):
        rows = pl.ds(k * couples, couples)

        @pl.when(half == 1)
        def _():
            s.back_in[rows] = jnp.zeros((couples, 2, count * groups, BLOCK), F32)

        @pl.when(half == 0)
        def _():
            wait_for(s.back_in.at[rows], s.back_sem.at[k, 1])

        def complete(p, c):
            state = carried(split(s.leaving[p, full_rows - half_rows :]), s.back_in, p, False)
            s.leaving[p] = through(state, by_block(s.outflow[p]), p, False)

        over_couples(k, complete)

        def respond(p, c):
            grad = s.grad[p]
            drive_grad = product(two(grad), s.toeplitz[p], TURNED)
            drive_grad += product(two(s.leaving[p]), s.back[p], TURNED)
            drive_grad += scalar_rows(2, p) * grad
            norm_grad = drive_grad * s.mask[...]
            for i, value in enumerate((norm_grad * s.own_normed[p], norm_grad, grad * s.drive[p])):
                for side, line in enumerate(split(total_rows(value))):
                    s.part[k, pl.ds(4 * couples + i * own + 2 * c + side, 1), :] = line
            put_couple(c, norm_grad * scalar_rows(0, p))

        over_couples(k, respond)
        rows_out(s.d_out, k)
        for m in range(count):
            s.d_in[m, dp, k, pl.ds(here, 1)] = s.d_out[k, m, pl.ds(me, 1)]
            to_holders(s.d_out.at[k, m], s.d_in.at[m, :, k], s.d_sem.at[k, m])

    for k in range(HALVES):
        backward_first(k)
        if k == 0:
            sum_hop(1)
    for k in range(HALVES):
        backward_second(k)
    sum_hop(2)

    def sum_of_products(first, second):
        (a, b), (c, d) = (split(first), split(second))
        return (total_rows(a * c - b * d), total_rows(a * d + b * c))

    def correlate(p, c):
        drive, grad = (two(s.drive[p]), two(s.grad[p]))
        entering, leaving = (s.entering[p], s.leaving[p])
        second = dot(drive[0], s.down_ramp[p]) + dot(drive[1], s.down_ramp[p])
        third = dot(grad[0], s.base_ramp[p]) + dot(grad[1], s.base_ramp[p])
        moment = times(sum_of_products(entering, s.outflow[p]), power_of(0, p))
        paired = times(sum_of_products(leaving, entering), power_of(7, p))
        paired = (paired[0] * float(BLOCK), paired[1] * float(BLOCK))
        paired = plus(paired, plus(sum_of_products(leaving, second), sum_of_products(entering, third)))
        for i, line in enumerate(moment + paired):
            s.sums[i, pl.ds(p, 1), :] = line
        for side in range(2):
            lanes = slice(side * BLOCK, (side + 1) * BLOCK)
            left = over(drive[0][:, lanes], drive[1][:, lanes], drive[0][:, lanes])
            right = over(grad[0][:, lanes], grad[0][:, lanes], grad[1][:, lanes])
            cross = jnp.where(lane_id >= row_id, dot(left, right, SIDEWAYS), 0.0)
            lags = cross[:8]
            for i in range(1, BLOCK // 8):
                lags = lags + pltpu.roll(cross[8 * i : 8 * i + 8], BLOCK - 8 * i, 1)
            for bit in range(3):
                moved = pltpu.roll(lags, BLOCK - (1 << bit), 1)
                lags = jnp.where((row_id[:8] >> bit) & 1 == 1, moved, lags)
            s.lags[side, pl.ds(p, 1), :] = total_rows(lags)

    for k in range(HALVES):
        over_couples(k, correlate)

    def near(p, c):
        lags = [s.lags[side, pl.ds(p, 1), :] for side in range(2)]
        later = [jnp.where(row_lane < BLOCK - 1, pltpu.roll(line, BLOCK - 1, 1), 0.0) for line in lags]
        lags, later = (two(jnp.broadcast_to(beside(*lines), (8, 2 * BLOCK))) for lines in (lags, later))
        moment = product(lags, s.base[p])
        paired = dot(later[0], s.base_ramp[p]) + dot(later[1], s.base_ramp[p])
        for i, line in enumerate(split(moment[:1]) + split(paired[:1])):
            s.sums[i, pl.ds(p, 1), :] += line

    for k in range(HALVES):
        over_couples(k, near)
        for i in range(4):
            s.part[k, i * couples : (i + 1) * couples] = s.sums[i, k * couples : (k + 1) * couples]
    send(s.part.at[other], s.part_in, s.part_sem, partner)
    for m in range(count):
        result[m] = s.result[m].T
    sum_hop(3)

    def norm_backward(m):
        for k in range(HALVES):
            wait_for(s.d_out.at[k, m, pl.ds(0, members - 1)], s.d_sem.at[k, m, 1])
        inverse = s.inverse[m : m + 1]
        scaled = s.d_in[m].reshape(width, span)
        plain = jnp.zeros((1, span), F32)
        along = jnp.zeros((1, span), F32)
        for j in range(tiles):
            rows = slice(j * BLOCK, (j + 1) * BLOCK)
            piece = scaled[rows].astype(F32)
            plain += total_rows(piece)
            along += total_rows(piece * s.normed[m, rows])
        plain, along = (plain * (1.0 / width), along * (1.0 / width))
        for j in range(tiles):
            rows = slice(j * BLOCK, (j + 1) * BLOCK)
            piece = scaled[rows].astype(F32) - plain - s.normed[m, rows] * along
            piece = s.upstream[m, rows].astype(F32) + inverse * piece
            token_grad[m, :, rows] = piece.astype(BF16).T

    norm_backward(0)

    wait_for(s.part_in, s.part_sem.at[0])
    wait_for(s.part_in, s.part_sem.at[1])
    mine = s.part[half] + s.part_in[...]
    moment, paired = (
        tuple(mine[i * couples : (i + 1) * couples] for i in pick) for pick in ((0, 1), (2, 3))
    )
    parts_own, pull = jax.vjp(coefficient_parts, *raw_params(half))
    paired = times(paired, parts_own[2:])
    grads = pull((paired[0], -paired[1], moment[0], -moment[1]))

    def uncoupled(value):
        s.turn[pl.ds(0, couples, stride=2), :] = value
        s.turn[pl.ds(1, couples, stride=2), :] = pltpu.roll(value, states, 1)
        return s.turn[...]

    rate_grad[...] = uncoupled(grads[0])[:, :states]
    turn_grad[...] = uncoupled(grads[1])[:, :states]
    mix_low = own_lane < states
    mix_re = uncoupled(grads[3])
    mixing_grad[...] = jnp.where(mix_low, mix_re, pltpu.roll(uncoupled(grads[4]), states, 1))
    lines = [jnp.where(mix_low, uncoupled(grads[2]), 0.0)]
    lines += [mine[4 * couples + i * own : 4 * couples + (i + 1) * own] for i in range(3)]
    ones = jnp.ones((8, BLOCK), F32)
    for rows, out in zip(lines, (spacing_grad, gain_grad, bias_grad, skip_grad), strict=True):
        line = lax.dot_general(ones, rows, (TURNED, ((), ())), preferred_element_type=F32, precision=HIGH)
        out[...] = line[:1]

    for m in range(1, count):
        norm_backward(m)

    wait_for(many(s.note_in), s.note_sem.at[0])
    for m in range(count):
        wait_for(many(s.scale_in.at[m]), s.scale_sem.at[m, 0])
        for k in range(HALVES):
            wait_for(many(s.x_in.at[k, m]), s.x_sem.at[k, m, 0])
            wait_for(many(s.a_out.at[k, m]), s.a_sem.at[k, m, 0])
            wait_for(many(s.g_in.at[k, m]), s.g_sem.at[k, m, 0])
            wait_for(many(s.d_out.at[k, m]), s.d_sem.at[k, m, 0])
    for k in range(HALVES):
        rows = pl.ds(k * couples, couples)

        @pl.when(half == 0)
        def _():
            wait_for(s.carry_out.at[rows], s.carry_sem.at[k, 0])

        @pl.when(half == 1)
        def _():
            wait_for(s.back_out.at[rows], s.back_sem.at[k, 0])


class Scratch:
    def __init__(self, names, refs):
        for name, ref in zip(names, refs, strict=True):
            setattr(self, name, ref)


def scratch_of(size, states):
    groups, parts, own, width, span, count = size
    local, blocks, zs = (parts // HALVES, span // BLOCK, parts // 2)
    members, couples = (groups * local, own // 2)
    every = HALVES * couples
    rows = blocks * count * members
    bits = 7 + (blocks * local).bit_length()
    wide = 2 * width + BLOCK
    vmem, sems = (pltpu.VMEM, pltpu.SemaphoreType.DMA)
    by_holder = (HALVES, count, groups, local, own, span)
    by_owner = (HALVES, count, members, own, span)
    filed = (count, groups, HALVES, local, own, span)
    chunk_sems = sems((HALVES, count, 2))
    held = vmem((every, rows, 2 * BLOCK), F32)
    table, plain = (vmem((every, 2, 2 * BLOCK, 2 * BLOCK), BF16), vmem((every, 2 * BLOCK, 2 * BLOCK), BF16))
    carry = vmem((every, 2, count * groups, BLOCK), F32)
    part_rows = 4 * couples + 3 * own
    return {
        "tokens": vmem((count, width, span), BF16),
        "upstream": vmem((count, width, span), BF16),
        "result": vmem((count, width, span), BF16),
        "normed": vmem((count, width, span), F32),
        "inverse": vmem((count, span), F32),
        "valid": vmem((count, span), F32),
        "x_out": vmem(by_holder, I16), "x_in": vmem(by_owner, I16), "x_sem": chunk_sems,
        "a_out": vmem(by_owner, BF16), "a_in": vmem(filed, BF16), "a_sem": chunk_sems,
        "g_out": vmem(by_holder, I16), "g_in": vmem(by_owner, I16), "g_sem": chunk_sems,
        "d_out": vmem(by_owner, BF16), "d_in": vmem(filed, BF16), "d_sem": chunk_sems,
        "note_out": vmem((1, 1, BLOCK), F32), "note_in": vmem((members, 1, BLOCK), F32), "note_sem": sems((2,)),
        "scale_out": vmem((count, 1, BLOCK), F32), "scale_in": vmem((count, members, 1, BLOCK), F32),
        "scale_sem": sems((count, 2)),
        "scales": vmem((rows, 2 * BLOCK), F32),
        "params": vmem((HALVES, own, 3 * BLOCK), F32), "params_sem": sems((2,)),
        "weight_out": vmem((own, wide), BF16),
        "weight": vmem((groups, zs, 2, own, wide), BF16), "weight_sem": sems((3, 2)),
        "flat": vmem((width, 2 * width), BF16),
        "flipped": vmem((2 * width, width), BF16),
        "shift": vmem((2 * width, BLOCK), F32),
        "pre_grad": vmem((2 * width, span), BF16),
        "act_grad": vmem((width, span), F32),
        "total": vmem((groups, zs, 2, own, wide), F32),
        "sum_core": vmem((groups, zs, own, wide), F32),
        "sum_dp_out": vmem((groups, zs, own, wide), BF16),
        "sum_dp_in": vmem((groups, zs, own, wide), BF16),
        "sum_z_out": vmem((zs, own, wide), BF16),
        "sum_z_in": vmem((zs, own, wide), BF16),
        "sum_sem": sems((3, 2)),
        "turn": vmem((own, BLOCK), F32),
        "scalars": vmem((3, HALVES * own, BLOCK), F32),
        "power": vmem((bits, 2, every, BLOCK), F32),
        "lead": vmem((2, every, BLOCK), F32),
        "coeff": vmem((2, every, BLOCK), F32),
        "base": table, "down": table, "up": table, "back": table, "toeplitz": table,
        "base_ramp": plain, "down_ramp": plain,
        "stage_in": vmem((blocks, count, members * own, BLOCK), F32),
        "stage_out": vmem((blocks, count, members * own, BLOCK), F32),
        "mask": vmem((rows, 2 * BLOCK), F32),
        "own_normed": held, "drive": held, "entering": held, "slope": held, "inflow": held,
        "grad": held, "outflow": held, "leaving": held,
        "widen": vmem((every, 2, count * members, BLOCK), F32),
        "carry_out": carry, "carry_in": carry, "carry_sem": sems((HALVES, 2)),
        "back_out": carry, "back_in": carry, "back_sem": sems((HALVES, 2)),
        "sums": vmem((4, every, BLOCK), F32),
        "lags": vmem((2, every, BLOCK), F32),
        "part": vmem((HALVES, part_rows, BLOCK), F32), "part_in": vmem((part_rows, BLOCK), F32),
        "part_sem": sems((2,)),
    }


def handed_over(values):
    def kernel(*refs):
        for given, out in zip(refs[: len(values)], refs[len(values) :], strict=True):
            out[...] = given[...].reshape(out.shape)

    shapes = [(value.size,) if value.shape[0] == 1 else value.shape for value in values]
    return pl.pallas_call(
        kernel,
        out_shape=[jax.ShapeDtypeStruct(shape, value.dtype) for shape, value in zip(shapes, values, strict=True)],
        in_specs=[pl.BlockSpec(memory_space=pltpu.VMEM)] * len(values),
        out_specs=[pl.BlockSpec(memory_space=pltpu.VMEM)] * len(values),
    )(*values)


def in_one_kernel(groups, parts, *args):
    inputs, lengths, ln_gain, ln_bias, lam_log, lam_im, log_dt, mix_weight, skip, glu_weight, glu_bias, out_grad = args
    count, span, width = inputs.shape
    own = ln_gain.shape[0]
    size = (groups, parts, own, width, span, count)
    scratch = scratch_of(size, lam_log.shape[1])

    def kernel(*refs):
        arguments, results, kept = (refs[:12], refs[12:23], refs[23:])
        whole_kernel(size, *arguments, *results, Scratch(scratch, kept))

    vmem, smem = (pl.BlockSpec(memory_space=pltpu.VMEM), pl.BlockSpec(memory_space=pltpu.SMEM))
    line = jax.ShapeDtypeStruct((1, own), F32)
    outs = pl.pallas_call(
        kernel,
        out_shape=(
            jax.ShapeDtypeStruct(inputs.shape, BF16),
            jax.ShapeDtypeStruct(inputs.shape, BF16),
            line,
            line,
            jax.ShapeDtypeStruct(lam_log.shape, F32),
            jax.ShapeDtypeStruct(lam_im.shape, F32),
            line,
            jax.ShapeDtypeStruct(mix_weight.shape, F32),
            line,
            jax.ShapeDtypeStruct(glu_weight.shape, F32),
            jax.ShapeDtypeStruct((1, 2 * own), F32),
        ),
        in_specs=[vmem, smem, smem, smem, vmem, vmem, smem, vmem, smem, vmem, smem, vmem],
        out_specs=[vmem] * 11,
        scratch_shapes=list(scratch.values()),
        compiler_params=pltpu.CompilerParams(
            collective_id=0, has_side_effects=True, vmem_limit_bytes=62 * 1024 * 1024
        ),
    )(*args)
    return tuple(handed_over(outs))


def solution(mesh):
    tokens, vector, matrix = (P("dp", "seq", None), P(BOTH), P(BOTH, None))
    groups, parts = (mesh.shape["dp"], mesh.shape["seq"])

    def step(*args):
        own = args[2].shape[0]
        if own % 16 == 0 and parts % 4 == 0:
            return in_one_kernel(groups, parts, *args)
        return per_device(*args)

    return jax.shard_map(
        step,
        mesh=mesh,
        in_specs=(
            tokens, P("dp"), vector, vector, matrix, matrix, vector, matrix, vector, matrix, vector, tokens,
        ),
        out_specs=(
            tokens, tokens, vector, vector, matrix, matrix, vector, matrix, vector, matrix, vector,
        ),
        check_vma=False,
    )
```

profile of v0, /device:TPU:0, one launch (start us, length us, event | category | flops | bytes accessed | tf_op | source)
XLA Modules:
  0.0 70.7 jit_solution(6770458998578194840)
XLA Ops:
  0.6 67.6 %shard_map.203 = (bf16[2,256,512]{2,1,0:T(8,128)(2,1)}, bf16[2,256,512]{2,1,0:T(8,128)(2,1)}, f32[1,16]{1,0:T(1,128)}, f32[1,16]{1,0:T(1,128)}, f32[16,64]{1,0:T...) custom-call(bf16[2,256,512]{2,1,0:T(8,128)(2,1)} %refs_0_.1, ...), custom_call_target="tpu_custom_call" | custom-call | tf_op jit(solution)/shard_map/pallas_call | solution.py:1130
  68.2 2.3 %shard_map.204 = (bf16[2,256,512]{2,1,0:T(8,128)(2,1)}, bf16[2,256,512]{2,1,0:T(8,128)(2,1)}, f32[16]{0:T(128)}, f32[16]{0:T(128)}, f32[16,64]{1,0:T(8,128)}, /*...) custom-call(bf16[2,256,512]{2,1,0:T(8,128)(2,1)} %get-tuple-element., ...), custom_call_target="tpu_custom_call" | custom-call | tf_op jit(solution)/shard_map/pallas_call | solution.py:1109
where the time goes:
time: 70.9 us; the launch traced here: 70.7 us
  Pallas kernels  69.9 us (99%)
  between operations  0.81 us (1%)
    pallas_call x1, Pallas kernels, in_one_kernel(): pl.pallas_call(kernel, out_shape=(jax.ShapeDtypeStruct(inputs.shape, BF16...  67.6 us
    pallas_call x1, Pallas kernels, handed_over(): pl.pallas_call(kernel, out_shape=[jax.ShapeDtypeStruct(shape, value.dtype...  2.33 us

commit v1 on v0

--- a/solution.py
+++ b/solution.py
@@ -229,7 +229,13 @@
 
 
 def product(left, table, dims=((1,), (0,))):
-    return dot(left[0], table[0], dims) + dot(left[1], table[0], dims) + dot(left[0], table[1], dims)
+    return folded(over(*left), table[0], dims) + dot(left[0], table[1], dims)
+
+
+def folded(rows, table, dims=((1,), (0,))):
+    value = dot(rows, table, dims)
+    half = value.shape[0] // 2
+    return value[:half] + value[half:]
 
 
 def times(value, factor):
@@ -316,27 +322,18 @@
         pltpu.make_async_copy(ref, ref, sem).wait()
 
     def to_owners(out, into, sems):
-        def one(k, carry):
+        for k in range(1, members):
             member = lax.rem(me + k, members)
             send(out.at[member // local, lax.rem(member, local)], into.at[me], sems, place(member))
-            return carry
-
-        lax.fori_loop(1, members, one, 0)
 
     def to_holders(out, into, sems):
-        def one(k, carry):
+        for k in range(1, members):
             member = lax.rem(me + k, members)
             send(out.at[member], into.at[dp, here], sems, place(member))
-            return carry
-
-        lax.fori_loop(1, members, one, 0)
 
     def to_all(out, into, sems):
-        def one(k, carry):
+        for k in range(1, members):
             send(out, into.at[me], sems, place(lax.rem(me + k, members)))
-            return carry
-
-        lax.fori_loop(1, members, one, 0)
 
     def many(ref):
         return ref.at[pl.ds(0, members - 1)]
@@ -386,9 +383,6 @@
         for k in range(HALVES):
             s.x_in[k, m, pl.ds(me, 1)] = s.x_out[k, m, dp, pl.ds(here, 1)]
 
-    for m in range(count):
-        norm(m)
-
     row_lane = lax.broadcasted_iota(jnp.int32, (1, BLOCK), 1)
     row = jnp.zeros((1, BLOCK), F32)
     for m in range(count):
@@ -445,10 +439,11 @@
     pl.semaphore_wait(barrier, members - 1 + zs // HALVES)
     send(s.params.at[half], s.params.at[half], s.params_sem, partner)
     to_all(s.note_out.at[0], s.note_in, s.note_sem)
-    for k in range(HALVES):
-        for m in range(count):
+    weight_hop(0)
+    for m in range(count):
+        norm(m)
+        for k in range(HALVES):
             to_owners(s.x_out.at[k, m], s.x_in.at[k, m], s.x_sem.at[k, m])
-    weight_hop(0)
 
     wait_for(s.params.at[0], s.params_sem.at[0])
     wait_for(s.params.at[0], s.params_sem.at[1])
@@ -473,8 +468,10 @@
         rest = s.params[k, :, 2 * BLOCK :]
         for i in range(1, 4):
             s.scalars[i - 1, k * own : (k + 1) * own] = jnp.broadcast_to(rest[:, i : i + 1], (own, BLOCK))
-        parts_k = coefficient_parts(*raw_params(k))
         rows = slice(k * couples, (k + 1) * couples)
+        for i, value in enumerate(raw_params(k)):
+            s.raw[i, rows] = value
+        parts_k = coefficient_parts(*(s.raw[i, rows] for i in range(5)))
         decay, coeff = (parts_k[:2], parts_k[2:])
         s.coeff[0, rows], s.coeff[1, rows] = coeff
         s.lead[0, rows], s.lead[1, rows] = times(coeff, decay)
@@ -500,7 +497,7 @@
         for i, part in enumerate(two(beside(*value))):
             ref[p, i] = stacked(part)
 
-    def tables(p):
+    def tables_first(p):
         eight = row_id[:8]
         unit = (jnp.ones((8, BLOCK), F32), jnp.zeros((8, BLOCK), F32))
         base, down = (unit, unit)
@@ -513,17 +510,14 @@
             more, most = (times(base, step), times(down, step))
             base = (over(base[0], more[0]), over(base[1], more[1]))
             down = (over(most[0], down[0]), over(most[1], down[1]))
-        lead = (s.lead[0, pl.ds(p, 1), :], s.lead[1, pl.ds(p, 1), :])
-        up, back = (times(base, lead), times(down, lead))
-        put_table(s.base, p, base)
+        s.base_kept[p] = beside(*base)
+        s.down_kept[p] = beside(*down)
         put_table(s.down, p, down)
+
+    def tables_middle(p):
+        base = split(s.base_kept[p])
+        up = times(base, (s.lead[0, pl.ds(p, 1), :], s.lead[1, pl.ds(p, 1), :]))
         put_table(s.up, p, (up[0], -up[1]))
-        put_table(s.back, p, (back[0], -back[1]))
-        for ref, value, slope in (
-            (s.base_ramp, base, ramp + 1.0),
-            (s.down_ramp, down, BLOCK - 1.0 - ramp),
-        ):
-            ref[p] = stacked(beside(value[0] * slope, value[1] * slope).astype(BF16))
         weights = beside(s.coeff[0, pl.ds(p, 1), :], -s.coeff[1, pl.ds(p, 1), :])
         weights = jnp.broadcast_to(weights, (8, 2 * BLOCK))
         pick = lax.rem(lax.broadcasted_iota(jnp.int32, (8, 2 * BLOCK), 1), BLOCK) < states
@@ -541,6 +535,17 @@
                 s.toeplitz[p, part, side, side] = value
                 s.toeplitz[p, part, side, off] = jnp.zeros(square, BF16)
 
+    def tables_second(p):
+        base, down = (split(s.base_kept[p]), split(s.down_kept[p]))
+        back = times(down, (s.lead[0, pl.ds(p, 1), :], s.lead[1, pl.ds(p, 1), :]))
+        put_table(s.base, p, base)
+        put_table(s.back, p, (back[0], -back[1]))
+        for ref, value, slope in (
+            (s.base_ramp, base, ramp + 1.0),
+            (s.down_ramp, down, BLOCK - 1.0 - ramp),
+        ):
+            ref[p] = stacked(beside(value[0] * slope, value[1] * slope).astype(BF16))
+
     def over_couples(k, body, group=GROUP):
         def some(g, carry):
             for u in range(group):
@@ -550,7 +555,7 @@
         lax.fori_loop(0, couples // group, some, 0)
 
     for k in range(HALVES):
-        over_couples(k, lambda p, c: tables(p), 2)
+        over_couples(k, lambda p, c: tables_first(p))
 
     half_rows = count * members
     full_rows = blocks * half_rows
@@ -616,10 +621,13 @@
             reach *= 2
         return moved(total, 1), total
 
-    def carried(state, ref, p, upward):
+    def carried(state, ref, scales, p, c, k, upward):
+        scale = jnp.sum(jnp.where(carry_lane == c, scales[k], 0.0), axis=1, keepdims=True)
+        lines = ref[p].astype(F32)
+        lines = (lines[: count * groups] * scale, lines[count * groups :] * scale)
         for j in range(local):
             for i in range(2):
-                s.widen[p, i, pl.ds(j, count * groups, stride=local), :] = ref[p, i]
+                s.widen[p, i, pl.ds(j, count * groups, stride=local), :] = lines[i]
         carry = (s.widen[p, 0], s.widen[p, 1])
         distance = place_of if upward else local - 1 - place_of
         for bit in range(local.bit_length() - 1):
@@ -650,10 +658,18 @@
                 within = ((start + q * BLOCK).astype(F32) < length).astype(F32)
                 s.mask[first : first + members] = beside(within, within)
 
-    def pick_last(p, total, out, first):
+    carry_lane = lax.broadcasted_iota(jnp.int32, (count * groups, BLOCK), 1)
+
+    def pick_last(p, c, k, total, out, scales, first):
+        lines = []
         for i in range(2):
             s.widen[p, i] = total[i]
-            out[p, i] = s.widen[p, i, pl.ds(first, count * groups, stride=local), :]
+            lines.append(s.widen[p, i, pl.ds(first, count * groups, stride=local), :])
+        top = jnp.max(jnp.maximum(jnp.abs(lines[0]), jnp.abs(lines[1])), axis=1, keepdims=True)
+        top = jnp.maximum(top, 1e-30)
+        factor = STEPS / top
+        out[p] = jnp.round(over(lines[0] * factor, lines[1] * factor)).astype(I16)
+        scales[k] = jnp.where(carry_lane == c, top * (1.0 / STEPS), scales[k])
 
     def forward_first(k):
         for m in range(count):
@@ -669,44 +685,61 @@
 
         over_couples(k, inflow)
 
+        s.carry_scale_out[k] = jnp.zeros((count * groups, BLOCK), F32)
+
         def scanned(p, c):
             state, total = scan(by_block(s.inflow[p]), p, True)
             s.entering[p, :half_rows] = beside(*state)
-            pick_last(p, total, s.carry_out, local - 1)
+            pick_last(p, c, k, total, s.carry_out, s.carry_scale_out, local - 1)
 
         over_couples(k, scanned)
         rows = pl.ds(k * couples, couples)
 
         @pl.when(half == 0)
         def _():
-            send(s.carry_out.at[rows], s.carry_in.at[rows], s.carry_sem.at[k], partner)
+            send(s.carry_out.at[rows], s.carry_in.at[rows], s.carry_sem.at[k, 0], partner)
+            send(s.carry_scale_out.at[k], s.carry_scale_in.at[k], s.carry_sem.at[k, 1], partner)
+
+    def forward_local(k):
+        def nearby(p, c):
+            drive = s.drive[p]
+            s.response[p] = product(two(drive), s.toeplitz[p]) + scalar_rows(2, p) * drive
+
+        over_couples(k, nearby)
+
+    def share_below(response):
+        return 0.5 * (1.0 + lax.erf(response * math.sqrt(0.5)))
+
+    def slopes(p, c):
+        response = s.response[p]
+        density = jnp.exp(-0.5 * response * response) * (1.0 / math.sqrt(2.0 * math.pi))
+        s.slope[p] = share_below(response) + response * density
 
     def forward_second(k):
         rows = pl.ds(k * couples, couples)
 
         @pl.when(half == 0)
         def _():
-            s.carry_in[rows] = jnp.zeros((couples, 2, count * groups, BLOCK), F32)
+            s.carry_in[rows] = jnp.zeros((couples, 2 * count * groups, BLOCK), I16)
+            s.carry_scale_in[k] = jnp.zeros((count * groups, BLOCK), F32)
 
         @pl.when(half == 1)
         def _():
-            wait_for(s.carry_in.at[rows], s.carry_sem.at[k, 1])
+            wait_for(s.carry_in.at[rows], s.carry_sem.at[k, 0, 1])
+            wait_for(s.carry_scale_in.at[k], s.carry_sem.at[k, 1, 1])
 
         def complete(p, c):
-            state = carried(split(s.entering[p, :half_rows]), s.carry_in, p, True)
+            state = carried(
+                split(s.entering[p, :half_rows]), s.carry_in, s.carry_scale_in, p, c, k, True
+            )
             s.entering[p] = through(state, by_block(s.inflow[p]), p, True)
 
         over_couples(k, complete)
 
         def respond(p, c):
-            drive = s.drive[p]
-            response = product(two(drive), s.toeplitz[p])
-            response += product(two(s.entering[p]), s.up[p], TURNED)
-            response += scalar_rows(2, p) * drive
-            share_below = 0.5 * (1.0 + lax.erf(response * math.sqrt(0.5)))
-            density = jnp.exp(-0.5 * response * response) * (1.0 / math.sqrt(2.0 * math.pi))
-            s.slope[p] = share_below + response * density
-            put_couple(c, response * share_below)
+            response = s.response[p] + product(two(s.entering[p]), s.up[p], TURNED)
+            s.response[p] = response
+            put_couple(c, response * share_below(response))
 
         over_couples(k, respond)
         rows_out(s.a_out, k)
@@ -715,16 +748,21 @@
             to_holders(s.a_out.at[k, m], s.a_in.at[m, :, k], s.a_sem.at[k, m])
 
     read_notes()
+    over_couples(0, lambda p, c: tables_middle(p))
+    weight_wait(0)
+    weight_hop(1)
+    over_couples(1, lambda p, c: tables_middle(p))
     for k in range(HALVES):
         forward_first(k)
-        if k == 0:
-            weight_wait(0)
-            weight_hop(1)
+    for k in range(HALVES):
+        forward_local(k)
     for k in range(HALVES):
         forward_second(k)
         if k == 0:
             weight_wait(1)
             weight_hop(2)
+    for k in range(HALVES):
+        over_couples(k, lambda p, c: tables_second(p))
 
     for m in range(count):
         s.upstream[m] = out_grad[m].T
@@ -749,20 +787,21 @@
             wait_for(ref, s.a_sem.at[k, m, 1])
         activated = s.a_in[m].reshape(width, span)
         valid = s.valid[m : m + 1]
+        lanes = slice(m * span, (m + 1) * span)
+        s.pre[...] = dot(s.flipped[...], activated)
         for j in range(tiles):
             rows = slice(j * BLOCK, (j + 1) * BLOCK)
             gates = slice(width + j * BLOCK, width + (j + 1) * BLOCK)
-            value = dot(s.flipped[rows], activated) + beside(*[s.shift[rows]] * blocks)
-            gate = jax.nn.sigmoid(dot(s.flipped[gates], activated) + beside(*[s.shift[gates]] * blocks))
+            value = s.pre[rows] + beside(*[s.shift[rows]] * blocks)
+            gate = jax.nn.sigmoid(s.pre[gates] + beside(*[s.shift[gates]] * blocks))
             gated = s.upstream[m, rows].astype(F32) * valid
-            s.pre_grad[rows] = (gated * gate).astype(BF16)
-            s.pre_grad[gates] = (gated * value * gate * (1.0 - gate)).astype(BF16)
+            s.pre_grad[rows, lanes] = (gated * gate).astype(BF16)
+            s.pre_grad[gates, lanes] = (gated * value * gate * (1.0 - gate)).astype(BF16)
             s.result[m, rows] = (s.tokens[m, rows].astype(F32) + value * gate * valid).astype(BF16)
+        s.act_grad[...] = dot(s.flat[...], s.pre_grad[:, lanes])
         largest = jnp.zeros((1, 1), F32)
         for j in range(tiles):
-            rows = slice(j * BLOCK, (j + 1) * BLOCK)
-            piece = dot(s.flat[rows], s.pre_grad[...])
-            s.act_grad[rows] = piece
+            piece = s.act_grad[j * BLOCK : (j + 1) * BLOCK]
             largest = jnp.maximum(largest, jnp.max(jnp.abs(piece), axis=(0, 1), keepdims=True))
         largest = jnp.maximum(largest, 1e-30)
         s.scale_out[m] = jnp.broadcast_to(largest * (1.0 / STEPS), (1, BLOCK))
@@ -776,35 +815,34 @@
         for k in range(HALVES):
             s.g_in[k, m, pl.ds(me, 1)] = s.g_out[k, m, dp, pl.ds(here, 1)]
             to_owners(s.g_out.at[k, m], s.g_in.at[k, m], s.g_sem.at[k, m])
-        ones = jnp.ones((span, BLOCK), BF16)
+    def weight_gradient():
+        ones = jnp.ones((count * span, BLOCK), BF16)
+        per = width // groups
+        lane4 = lax.broadcasted_iota(jnp.int32, (zs, 2, own, BLOCK), 3)
         for j in range(groups):
-            per = width // groups
-            rows = slice(j * per, (j + 1) * per)
-            piece = dot(activated[rows], s.pre_grad[...], TURNED).reshape(zs, 2, own, wide)
+            activated = beside(*(s.a_in[m, j].reshape(per, span) for m in range(count)))
+            piece = dot(activated, s.pre_grad[...], TURNED).reshape(zs, 2, own, wide)
             sums = dot(s.pre_grad[2 * j * per : 2 * (j + 1) * per], ones).reshape(zs, 2, 2, own, BLOCK)
-            lane4 = lax.broadcasted_iota(jnp.int32, (zs, 2, own, BLOCK), 3)
             sums = jnp.where(lane4 == 0, sums[:, :, 0], jnp.where(lane4 == 1, sums[:, :, 1], 0.0))
-            if m == 0:
-                s.total[j, :, :, :, :wide] = piece
-                s.total[j, :, :, :, wide:] = sums
-            else:
-                s.total[j, :, :, :, :wide] += piece
-                s.total[j, :, :, :, wide:] += sums
+            s.total[j, :, :, :, :wide] = piece
+            s.total[j, :, :, :, wide:] = sums
 
     for m in range(count):
         project(m)
+    weight_gradient()
 
     def sum_hop(hop):
         sems = s.sum_sem
         if hop == 0:
             send(s.total.at[:, :, 1 - core], s.sum_core, sems.at[0], (dp, z * 2 + 1 - core))
-        elif hop == 1:
+        elif hop == "ready":
             wait_for(s.sum_core, sems.at[0, 0])
             wait_for(s.sum_core, sems.at[0, 1])
             for j in range(groups):
                 part = s.total[j, :, pl.ds(core, 1)].reshape(zs, own, -1) + s.sum_core[j]
                 s.sum_core[j] = part
                 s.sum_dp_out[j] = part.astype(BF16)
+        elif hop == 1:
             for k in range(1, groups):
                 there = lax.rem(dp + k, groups)
                 send(s.sum_dp_out.at[there], s.sum_dp_in.at[dp], sems.at[1], (there, seq))
@@ -832,6 +870,9 @@
             shift_grad[...] = beside(columns[:1], columns[1:2])
 
     sum_hop(0)
+    for k in range(HALVES):
+        over_couples(k, slopes)
+    sum_hop("ready")
 
     def backward_first(k):
         for m in range(count):
@@ -842,6 +883,8 @@
                 for q in range(blocks):
                     first = (q * count + m) * members
                     s.scales[first : first + members] = beside(scale, scale)
+        if k == 0:
+            sum_hop(1)
         rows_in(s.g_in, k)
 
         def outflow(p, c):
@@ -851,44 +894,56 @@
 
         over_couples(k, outflow)
 
+        s.back_scale_out[k] = jnp.zeros((count * groups, BLOCK), F32)
+
         def scanned(p, c):
             state, total = scan(by_block(s.outflow[p]), p, False)
             s.leaving[p, full_rows - half_rows :] = beside(*state)
-            pick_last(p, total, s.back_out, 0)
+            pick_last(p, c, k, total, s.back_out, s.back_scale_out, 0)
 
         over_couples(k, scanned)
         rows = pl.ds(k * couples, couples)
 
         @pl.when(half == 1)
         def _():
-            send(s.back_out.at[rows], s.back_in.at[rows], s.back_sem.at[k], partner)
+            send(s.back_out.at[rows], s.back_in.at[rows], s.back_sem.at[k, 0], partner)
+            send(s.back_scale_out.at[k], s.back_scale_in.at[k], s.back_sem.at[k, 1], partner)
+
+    def backward_local(k):
+        def nearby(p, c):
+            grad = s.grad[p]
+            s.response[p] = product(two(grad), s.toeplitz[p], TURNED) + scalar_rows(2, p) * grad
+
+        over_couples(k, nearby)
 
     def backward_second(k):
         rows = pl.ds(k * couples, couples)
 
         @pl.when(half == 1)
         def _():
-            s.back_in[rows] = jnp.zeros((couples, 2, count * groups, BLOCK), F32)
+            s.back_in[rows] = jnp.zeros((couples, 2 * count * groups, BLOCK), I16)
+            s.back_scale_in[k] = jnp.zeros((count * groups, BLOCK), F32)
 
         @pl.when(half == 0)
         def _():
-            wait_for(s.back_in.at[rows], s.back_sem.at[k, 1])
+            wait_for(s.back_in.at[rows], s.back_sem.at[k, 0, 1])
+            wait_for(s.back_scale_in.at[k], s.back_sem.at[k, 1, 1])
 
         def complete(p, c):
-            state = carried(split(s.leaving[p, full_rows - half_rows :]), s.back_in, p, False)
+            state = carried(
+                split(s.leaving[p, full_rows - half_rows :]), s.back_in, s.back_scale_in, p, c, k, False
+            )
             s.leaving[p] = through(state, by_block(s.outflow[p]), p, False)
 
         over_couples(k, complete)
 
         def respond(p, c):
             grad = s.grad[p]
-            drive_grad = product(two(grad), s.toeplitz[p], TURNED)
-            drive_grad += product(two(s.leaving[p]), s.back[p], TURNED)
-            drive_grad += scalar_rows(2, p) * grad
+            drive_grad = s.response[p] + product(two(s.leaving[p]), s.back[p], TURNED)
             norm_grad = drive_grad * s.mask[...]
             for i, value in enumerate((norm_grad * s.own_normed[p], norm_grad, grad * s.drive[p])):
                 for side, line in enumerate(split(total_rows(value))):
-                    s.part[k, pl.ds(4 * couples + i * own + 2 * c + side, 1), :] = line
+                    s.part[k, pl.ds(5 * couples + i * own + 2 * c + side, 1), :] = line
             put_couple(c, norm_grad * scalar_rows(0, p))
 
         over_couples(k, respond)
@@ -899,8 +954,8 @@
 
     for k in range(HALVES):
         backward_first(k)
-        if k == 0:
-            sum_hop(1)
+    for k in range(HALVES):
+        backward_local(k)
     for k in range(HALVES):
         backward_second(k)
     sum_hop(2)
@@ -909,17 +964,9 @@
         (a, b), (c, d) = (split(first), split(second))
         return (total_rows(a * c - b * d), total_rows(a * d + b * c))
 
-    def correlate(p, c):
+    def lag_sums(p, c):
         drive, grad = (two(s.drive[p]), two(s.grad[p]))
-        entering, leaving = (s.entering[p], s.leaving[p])
-        second = dot(drive[0], s.down_ramp[p]) + dot(drive[1], s.down_ramp[p])
-        third = dot(grad[0], s.base_ramp[p]) + dot(grad[1], s.base_ramp[p])
-        moment = times(sum_of_products(entering, s.outflow[p]), power_of(0, p))
-        paired = times(sum_of_products(leaving, entering), power_of(7, p))
-        paired = (paired[0] * float(BLOCK), paired[1] * float(BLOCK))
-        paired = plus(paired, plus(sum_of_products(leaving, second), sum_of_products(entering, third)))
-        for i, line in enumerate(moment + paired):
-            s.sums[i, pl.ds(p, 1), :] = line
+        lines = []
         for side in range(2):
             lanes = slice(side * BLOCK, (side + 1) * BLOCK)
             left = over(drive[0][:, lanes], drive[1][:, lanes], drive[0][:, lanes])
@@ -931,28 +978,43 @@
             for bit in range(3):
                 moved = pltpu.roll(lags, BLOCK - (1 << bit), 1)
                 lags = jnp.where((row_id[:8] >> bit) & 1 == 1, moved, lags)
-            s.lags[side, pl.ds(p, 1), :] = total_rows(lags)
-
+            lines.append(total_rows(lags))
+        later = [jnp.where(row_lane < BLOCK - 1, pltpu.roll(line, BLOCK - 1, 1), 0.0) for line in lines]
+        eight = lax.broadcasted_iota(jnp.int32, (8, 2 * BLOCK), 0)
+        near = jnp.where(eight == 0, beside(*(line * shrink for line in lines)), beside(*later))
+        s.lags[p] = near
+
+    def correlate(p, c):
+        drive, grad, near = (two(s.drive[p]), two(s.grad[p]), two(s.lags[p]))
+        entering, leaving = (s.entering[p], s.leaving[p])
+        second = folded(over(*drive), s.down_ramp[p])
+        third = dot(over(*grad, *near), s.base_ramp[p])
+        near = third[2 * full_rows : 2 * full_rows + 8] + third[2 * full_rows + 8 :]
+        third = third[:full_rows] + third[full_rows : 2 * full_rows]
+        moment = times(sum_of_products(entering, s.outflow[p]), power_of(0, p))
+        moment = plus(moment, split(near[:1]))
+        paired = times(sum_of_products(leaving, entering), power_of(7, p))
+        paired = (paired[0] * float(BLOCK), paired[1] * float(BLOCK))
+        paired = plus(paired, plus(sum_of_products(leaving, second), sum_of_products(entering, third)))
+        paired = plus(paired, split(near[1:2]))
+        for i, line in enumerate(moment + paired):
+            s.sums[i, pl.ds(p, 1), :] = line
+
+    shrink = 1.0 / (row_lane.astype(F32) + 1.0)
+    for k in range(HALVES):
+        over_couples(k, lag_sums)
     for k in range(HALVES):
         over_couples(k, correlate)
-
-    def near(p, c):
-        lags = [s.lags[side, pl.ds(p, 1), :] for side in range(2)]
-        later = [jnp.where(row_lane < BLOCK - 1, pltpu.roll(line, BLOCK - 1, 1), 0.0) for line in lags]
-        lags, later = (two(jnp.broadcast_to(beside(*lines), (8, 2 * BLOCK))) for lines in (lags, later))
-        moment = product(lags, s.base[p])
-        paired = dot(later[0], s.base_ramp[p]) + dot(later[1], s.base_ramp[p])
-        for i, line in enumerate(split(moment[:1]) + split(paired[:1])):
-            s.sums[i, pl.ds(p, 1), :] += line
-
-    for k in range(HALVES):
-        over_couples(k, near)
-        for i in range(4):
-            s.part[k, i * couples : (i + 1) * couples] = s.sums[i, k * couples : (k + 1) * couples]
+    raw = tuple(s.raw[i] for i in range(5))
+    moment, paired = ((s.sums[0], s.sums[1]), (s.sums[2], s.sums[3]))
+    paired = times(paired, (s.coeff[0], s.coeff[1]))
+    _, pull = jax.vjp(coefficient_parts, *raw)
+    for i, grad in enumerate(pull((paired[0], -paired[1], moment[0], -moment[1]))):
+        for k in range(HALVES):
+            s.part[k, i * couples : (i + 1) * couples] = grad[k * couples : (k + 1) * couples]
     send(s.part.at[other], s.part_in, s.part_sem, partner)
     for m in range(count):
         result[m] = s.result[m].T
-    sum_hop(3)
 
     def norm_backward(m):
         for k in range(HALVES):
@@ -973,17 +1035,13 @@
             piece = s.upstream[m, rows].astype(F32) + inverse * piece
             token_grad[m, :, rows] = piece.astype(BF16).T
 
-    norm_backward(0)
+    for m in range(count):
+        norm_backward(m)
 
     wait_for(s.part_in, s.part_sem.at[0])
     wait_for(s.part_in, s.part_sem.at[1])
     mine = s.part[half] + s.part_in[...]
-    moment, paired = (
-        tuple(mine[i * couples : (i + 1) * couples] for i in pick) for pick in ((0, 1), (2, 3))
-    )
-    parts_own, pull = jax.vjp(coefficient_parts, *raw_params(half))
-    paired = times(paired, parts_own[2:])
-    grads = pull((paired[0], -paired[1], moment[0], -moment[1]))
+    grads = [mine[i * couples : (i + 1) * couples] for i in range(5)]
 
     def uncoupled(value):
         s.turn[pl.ds(0, couples, stride=2), :] = value
@@ -996,14 +1054,13 @@
     mix_re = uncoupled(grads[3])
     mixing_grad[...] = jnp.where(mix_low, mix_re, pltpu.roll(uncoupled(grads[4]), states, 1))
     lines = [jnp.where(mix_low, uncoupled(grads[2]), 0.0)]
-    lines += [mine[4 * couples + i * own : 4 * couples + (i + 1) * own] for i in range(3)]
+    lines += [mine[5 * couples + i * own : 5 * couples + (i + 1) * own] for i in range(3)]
     ones = jnp.ones((8, BLOCK), F32)
     for rows, out in zip(lines, (spacing_grad, gain_grad, bias_grad, skip_grad), strict=True):
         line = lax.dot_general(ones, rows, (TURNED, ((), ())), preferred_element_type=F32, precision=HIGH)
         out[...] = line[:1]
 
-    for m in range(1, count):
-        norm_backward(m)
+    sum_hop(3)
 
     wait_for(many(s.note_in), s.note_sem.at[0])
     for m in range(count):
@@ -1018,11 +1075,13 @@
 
         @pl.when(half == 0)
         def _():
-            wait_for(s.carry_out.at[rows], s.carry_sem.at[k, 0])
+            wait_for(s.carry_out.at[rows], s.carry_sem.at[k, 0, 0])
+            wait_for(s.carry_scale_out.at[k], s.carry_sem.at[k, 1, 0])
 
         @pl.when(half == 1)
         def _():
-            wait_for(s.back_out.at[rows], s.back_sem.at[k, 0])
+            wait_for(s.back_out.at[rows], s.back_sem.at[k, 0, 0])
+            wait_for(s.back_scale_out.at[k], s.back_sem.at[k, 1, 0])
 
 
 class Scratch:
@@ -1046,8 +1105,10 @@
     chunk_sems = sems((HALVES, count, 2))
     held = vmem((every, rows, 2 * BLOCK), F32)
     table, plain = (vmem((every, 2, 2 * BLOCK, 2 * BLOCK), BF16), vmem((every, 2 * BLOCK, 2 * BLOCK), BF16))
-    carry = vmem((every, 2, count * groups, BLOCK), F32)
-    part_rows = 4 * couples + 3 * own
+    kept = vmem((every, BLOCK, 2 * BLOCK), F32)
+    carry, carry_sems = (vmem((every, 2 * count * groups, BLOCK), I16), sems((HALVES, 2, 2)))
+    carry_scale = vmem((HALVES, count * groups, BLOCK), F32)
+    part_rows = 5 * couples + 3 * own
     return {
         "tokens": vmem((count, width, span), BF16),
         "upstream": vmem((count, width, span), BF16),
@@ -1069,7 +1130,8 @@
         "flat": vmem((width, 2 * width), BF16),
         "flipped": vmem((2 * width, width), BF16),
         "shift": vmem((2 * width, BLOCK), F32),
-        "pre_grad": vmem((2 * width, span), BF16),
+        "pre_grad": vmem((2 * width, count * span), BF16),
+        "pre": vmem((2 * width, span), F32),
         "act_grad": vmem((width, span), F32),
         "total": vmem((groups, zs, 2, own, wide), F32),
         "sum_core": vmem((groups, zs, own, wide), F32),
@@ -1084,17 +1146,19 @@
         "lead": vmem((2, every, BLOCK), F32),
         "coeff": vmem((2, every, BLOCK), F32),
         "base": table, "down": table, "up": table, "back": table, "toeplitz": table,
-        "base_ramp": plain, "down_ramp": plain,
+        "base_ramp": plain, "down_ramp": plain, "base_kept": kept, "down_kept": kept, "response": held,
         "stage_in": vmem((blocks, count, members * own, BLOCK), F32),
         "stage_out": vmem((blocks, count, members * own, BLOCK), F32),
         "mask": vmem((rows, 2 * BLOCK), F32),
         "own_normed": held, "drive": held, "entering": held, "slope": held, "inflow": held,
         "grad": held, "outflow": held, "leaving": held,
         "widen": vmem((every, 2, count * members, BLOCK), F32),
-        "carry_out": carry, "carry_in": carry, "carry_sem": sems((HALVES, 2)),
-        "back_out": carry, "back_in": carry, "back_sem": sems((HALVES, 2)),
+        "carry_out": carry, "carry_in": carry, "carry_sem": carry_sems,
+        "back_out": carry, "back_in": carry, "back_sem": carry_sems,
+        "carry_scale_out": carry_scale, "carry_scale_in": carry_scale,
+        "back_scale_out": carry_scale, "back_scale_in": carry_scale,
         "sums": vmem((4, every, BLOCK), F32),
-        "lags": vmem((2, every, BLOCK), F32),
+        "raw": vmem((5, every, BLOCK), F32), "lags": vmem((every, 8, 2 * BLOCK), F32),
         "part": vmem((HALVES, part_rows, BLOCK), F32), "part_in": vmem((part_rows, BLOCK), F32),
         "part_sem": sems((2,)),
     }

time: 70.9 us -> 62.8 us (0.89)
  Pallas kernels: 69.9 us -> 61.9 us
    pallas_call x1, Pallas kernels: 67.6 us -> 59.5 us  [in_one_kernel(): pl.pallas_call(kernel, out_shape=(jax.ShapeDtypeStruct(inputs.shape, BF16...]
where the time goes in v1:
time: 62.8 us; the launch traced here: 62.7 us
  Pallas kernels  61.9 us (99%)
  between operations  0.81 us (1%)
    pallas_call x1, Pallas kernels, in_one_kernel(): pl.pallas_call(kernel, out_shape=(jax.ShapeDtypeStruct(inputs.shape, BF16...  59.5 us
    pallas_call x1, Pallas kernels, handed_over(): pl.pallas_call(kernel, out_shape=[jax.ShapeDtypeStruct(shape, value.dtype...  2.33 us

profile of v1, /device:TPU:0, one launch (start us, length us, event | category | flops | bytes accessed | tf_op | source)
XLA Modules:
  0.0 62.7 jit_solution(16894078990423071421)
XLA Ops:
  0.6 59.5 %shard_map.203 = (bf16[2,256,512]{2,1,0:T(8,128)(2,1)}, bf16[2,256,512]{2,1,0:T(8,128)(2,1)}, f32[1,16]{1,0:T(1,128)}, f32[1,16]{1,0:T(1,128)}, f32[16,64]{1,0:T...) custom-call(bf16[2,256,512]{2,1,0:T(8,128)(2,1)} %refs_0_.1, ...), custom_call_target="tpu_custom_call" | custom-call | tf_op jit(solution)/shard_map/pallas_call | solution.py:1194
  60.2 2.3 %shard_map.204 = (bf16[2,256,512]{2,1,0:T(8,128)(2,1)}, bf16[2,256,512]{2,1,0:T(8,128)(2,1)}, f32[16]{0:T(128)}, f32[16]{0:T(128)}, f32[16,64]{1,0:T(8,128)}, /*...) custom-call(bf16[2,256,512]{2,1,0:T(8,128)(2,1)} %get-tuple-element., ...), custom_call_target="tpu_custom_call" | custom-call | tf_op jit(solution)/shard_map/pallas_call | solution.py:1173

commit v2 on v1

--- a/solution.py
+++ b/solution.py
@@ -383,6 +383,11 @@
         for k in range(HALVES):
             s.x_in[k, m, pl.ds(me, 1)] = s.x_out[k, m, dp, pl.ds(here, 1)]
 
+    for p in range(HALVES * couples):
+        for part in range(2):
+            s.toeplitz[p, part, :BLOCK, BLOCK:] = jnp.zeros((BLOCK, BLOCK), BF16)
+            s.toeplitz[p, part, BLOCK:, :BLOCK] = jnp.zeros((BLOCK, BLOCK), BF16)
+
     row_lane = lax.broadcasted_iota(jnp.int32, (1, BLOCK), 1)
     row = jnp.zeros((1, BLOCK), F32)
     for m in range(count):
@@ -442,7 +447,8 @@
     weight_hop(0)
     for m in range(count):
         norm(m)
-        for k in range(HALVES):
+    for k in range(HALVES):
+        for m in range(count):
             to_owners(s.x_out.at[k, m], s.x_in.at[k, m], s.x_sem.at[k, m])
 
     wait_for(s.params.at[0], s.params_sem.at[0])
@@ -522,18 +528,14 @@
         weights = jnp.broadcast_to(weights, (8, 2 * BLOCK))
         pick = lax.rem(lax.broadcasted_iota(jnp.int32, (8, 2 * BLOCK), 1), BLOCK) < states
         pick = pick == (lax.broadcasted_iota(jnp.int32, (8, 2 * BLOCK), 0) == 0)
-        kernel = lax.dot_general(
-            jnp.where(pick, weights, 0.0), beside(*base), (TURNED, ((), ())),
-            preferred_element_type=F32, precision=HIGH,
-        )
+        weights, base = (two(jnp.where(pick, weights, 0.0)), two(beside(*base)))
+        kernel = folded(over(*weights), base[0], TURNED) + dot(weights[0], base[1], TURNED)
         for i in range(2):
             slanted = jnp.broadcast_to(kernel[i : i + 1], square)
             slanted = pltpu.roll(slanted, 0, 1, stride=1, stride_axis=0)
             side = slice(i * BLOCK, (i + 1) * BLOCK)
-            off = slice((1 - i) * BLOCK, (2 - i) * BLOCK)
             for part, value in enumerate(two(jnp.where(lane_id >= row_id, slanted, 0.0))):
                 s.toeplitz[p, part, side, side] = value
-                s.toeplitz[p, part, side, off] = jnp.zeros(square, BF16)
 
     def tables_second(p):
         base, down = (split(s.base_kept[p]), split(s.down_kept[p]))
@@ -873,6 +875,8 @@
     for k in range(HALVES):
         over_couples(k, slopes)
     sum_hop("ready")
+    for m in range(count):
+        result[m] = s.result[m].T
 
     def backward_first(k):
         for m in range(count):
@@ -1001,20 +1005,19 @@
             s.sums[i, pl.ds(p, 1), :] = line
 
     shrink = 1.0 / (row_lane.astype(F32) + 1.0)
-    for k in range(HALVES):
+    def parameters(k):
         over_couples(k, lag_sums)
-    for k in range(HALVES):
         over_couples(k, correlate)
-    raw = tuple(s.raw[i] for i in range(5))
-    moment, paired = ((s.sums[0], s.sums[1]), (s.sums[2], s.sums[3]))
-    paired = times(paired, (s.coeff[0], s.coeff[1]))
-    _, pull = jax.vjp(coefficient_parts, *raw)
-    for i, grad in enumerate(pull((paired[0], -paired[1], moment[0], -moment[1]))):
-        for k in range(HALVES):
-            s.part[k, i * couples : (i + 1) * couples] = grad[k * couples : (k + 1) * couples]
+        rows = pl.ds(pl.multiple_of(k * couples, couples), couples)
+        moment, paired = ((s.sums[0, rows], s.sums[1, rows]), (s.sums[2, rows], s.sums[3, rows]))
+        paired = times(paired, (s.coeff[0, rows], s.coeff[1, rows]))
+        _, pull = jax.vjp(coefficient_parts, *(s.raw[i, rows] for i in range(5)))
+        for i, grad in enumerate(pull((paired[0], -paired[1], moment[0], -moment[1]))):
+            s.part[pl.ds(k, 1), i * couples : (i + 1) * couples] = grad[None]
+
+    parameters(other)
     send(s.part.at[other], s.part_in, s.part_sem, partner)
-    for m in range(count):
-        result[m] = s.result[m].T
+    parameters(half)
 
     def norm_backward(m):
         for k in range(HALVES):

time: 62.8 us -> 59.6 us (0.949)
  Pallas kernels: 61.9 us -> 58.6 us
    pallas_call x1, Pallas kernels: 59.5 us -> 56.2 us  [in_one_kernel(): pl.pallas_call(kernel, out_shape=(jax.ShapeDtypeStruct(inputs.shape, BF16...]
where the time goes in v2:
time: 59.6 us; the launch traced here: 59.4 us
  Pallas kernels  58.6 us (98%)
  between operations  0.81 us (1%)
    pallas_call x1, Pallas kernels, in_one_kernel(): pl.pallas_call(kernel, out_shape=(jax.ShapeDtypeStruct(inputs.shape, BF16...  56.2 us
    pallas_call x1, Pallas kernels, handed_over(): pl.pallas_call(kernel, out_shape=[jax.ShapeDtypeStruct(shape, value.dtype...  2.33 us

profile of v2, /device:TPU:0, one launch (start us, length us, event | category | flops | bytes accessed | tf_op | source)
XLA Modules:
  0.0 59.4 jit_solution(11640231567001180588)
XLA Ops:
  0.6 56.2 %shard_map.203 = (bf16[2,256,512]{2,1,0:T(8,128)(2,1)}, bf16[2,256,512]{2,1,0:T(8,128)(2,1)}, f32[1,16]{1,0:T(1,128)}, f32[1,16]{1,0:T(1,128)}, f32[16,64]{1,0:T...) custom-call(bf16[2,256,512]{2,1,0:T(8,128)(2,1)} %refs_0_.1, ...), custom_call_target="tpu_custom_call" | custom-call | tf_op jit(solution)/shard_map/pallas_call | solution.py:1197
  56.9 2.3 %shard_map.204 = (bf16[2,256,512]{2,1,0:T(8,128)(2,1)}, bf16[2,256,512]{2,1,0:T(8,128)(2,1)}, f32[16]{0:T(128)}, f32[16]{0:T(128)}, f32[16,64]{1,0:T(8,128)}, /*...) custom-call(bf16[2,256,512]{2,1,0:T(8,128)(2,1)} %get-tuple-element., ...), custom_call_target="tpu_custom_call" | custom-call | tf_op jit(solution)/shard_map/pallas_call | solution.py:1176

commit v3 on v2

--- a/solution.py
+++ b/solution.py
@@ -456,7 +456,7 @@
     pair_low = lax.broadcasted_iota(jnp.int32, (couples, BLOCK), 1) < states
 
     def coupled(value):
-        s.turn[...] = value
+        s.turn[:own] = value
         even = s.turn[pl.ds(0, couples, stride=2), :]
         odd = s.turn[pl.ds(1, couples, stride=2), :]
         return jnp.where(pair_low, even, pltpu.roll(odd, states, 1))
@@ -569,13 +569,13 @@
         for m in range(count):
             for q in range(blocks):
                 piece = ref[k, m, :, :, q * BLOCK : (q + 1) * BLOCK]
-                s.stage_in[q, m] = piece.astype(F32).reshape(members * own, BLOCK)
+                s.stage_in[q, m, : members * own] = piece.astype(F32).reshape(members * own, BLOCK)
 
     def rows_out(ref, k):
         for m in range(count):
             for q in range(blocks):
                 ref[k, m, :, :, q * BLOCK : (q + 1) * BLOCK] = (
-                    s.stage_out[q, m].astype(BF16).reshape(members, own, BLOCK)
+                    s.stage_out[q, m, : members * own].astype(BF16).reshape(members, own, BLOCK)
                 )
 
     def gather_couple(c):
@@ -630,7 +630,7 @@
         for j in range(local):
             for i in range(2):
                 s.widen[p, i, pl.ds(j, count * groups, stride=local), :] = lines[i]
-        carry = (s.widen[p, 0], s.widen[p, 1])
+        carry = (s.widen[p, 0, :half_rows], s.widen[p, 1, :half_rows])
         distance = place_of if upward else local - 1 - place_of
         for bit in range(local.bit_length() - 1):
             further = times(carry, power_of(step_bit + bit, p))
@@ -665,7 +665,7 @@
     def pick_last(p, c, k, total, out, scales, first):
         lines = []
         for i in range(2):
-            s.widen[p, i] = total[i]
+            s.widen[p, i, :half_rows] = total[i]
             lines.append(s.widen[p, i, pl.ds(first, count * groups, stride=local), :])
         top = jnp.max(jnp.maximum(jnp.abs(lines[0]), jnp.abs(lines[1])), axis=1, keepdims=True)
         top = jnp.maximum(top, 1e-30)
@@ -1049,7 +1049,7 @@
     def uncoupled(value):
         s.turn[pl.ds(0, couples, stride=2), :] = value
         s.turn[pl.ds(1, couples, stride=2), :] = pltpu.roll(value, states, 1)
-        return s.turn[...]
+        return s.turn[:own]
 
     rate_grad[...] = uncoupled(grads[0])[:, :states]
     turn_grad[...] = uncoupled(grads[1])[:, :states]
@@ -1143,19 +1143,19 @@
         "sum_z_out": vmem((zs, own, wide), BF16),
         "sum_z_in": vmem((zs, own, wide), BF16),
         "sum_sem": sems((3, 2)),
-        "turn": vmem((own, BLOCK), F32),
+        "turn": vmem((own + 8, BLOCK), F32),
         "scalars": vmem((3, HALVES * own, BLOCK), F32),
         "power": vmem((bits, 2, every, BLOCK), F32),
         "lead": vmem((2, every, BLOCK), F32),
         "coeff": vmem((2, every, BLOCK), F32),
         "base": table, "down": table, "up": table, "back": table, "toeplitz": table,
         "base_ramp": plain, "down_ramp": plain, "base_kept": kept, "down_kept": kept, "response": held,
-        "stage_in": vmem((blocks, count, members * own, BLOCK), F32),
-        "stage_out": vmem((blocks, count, members * own, BLOCK), F32),
+        "stage_in": vmem((blocks, count, (members + 1) * own, BLOCK), F32),
+        "stage_out": vmem((blocks, count, (members + 1) * own, BLOCK), F32),
         "mask": vmem((rows, 2 * BLOCK), F32),
         "own_normed": held, "drive": held, "entering": held, "slope": held, "inflow": held,
         "grad": held, "outflow": held, "leaving": held,
-        "widen": vmem((every, 2, count * members, BLOCK), F32),
+        "widen": vmem((every, 2, count * members + 8, BLOCK), F32),
         "carry_out": carry, "carry_in": carry, "carry_sem": carry_sems,
         "back_out": carry, "back_in": carry, "back_sem": carry_sems,
         "carry_scale_out": carry_scale, "carry_scale_in": carry_scale,

time: 59.6 us -> 59.8 us (level)
  no operation moved by 1% of the time
where the time goes in v3:
time: 59.8 us; the launch traced here: 59.7 us
  Pallas kernels  58.9 us (98%)
  between operations  0.81 us (1%)
    pallas_call x1, Pallas kernels, in_one_kernel(): pl.pallas_call(kernel, out_shape=(jax.ShapeDtypeStruct(inputs.shape, BF16...  56.5 us
    pallas_call x1, Pallas kernels, handed_over(): pl.pallas_call(kernel, out_shape=[jax.ShapeDtypeStruct(shape, value.dtype...  2.33 us

profile of v3, /device:TPU:0, one launch (start us, length us, event | category | flops | bytes accessed | tf_op | source)
XLA Modules:
  0.0 59.7 jit_solution(12490295760988310129)
XLA Ops:
  0.6 56.5 %shard_map.203 = (bf16[2,256,512]{2,1,0:T(8,128)(2,1)}, bf16[2,256,512]{2,1,0:T(8,128)(2,1)}, f32[1,16]{1,0:T(1,128)}, f32[1,16]{1,0:T(1,128)}, f32[16,64]{1,0:T...) custom-call(bf16[2,256,512]{2,1,0:T(8,128)(2,1)} %refs_0_.1, ...), custom_call_target="tpu_custom_call" | custom-call | tf_op jit(solution)/shard_map/pallas_call | solution.py:1197
  57.2 2.3 %shard_map.204 = (bf16[2,256,512]{2,1,0:T(8,128)(2,1)}, bf16[2,256,512]{2,1,0:T(8,128)(2,1)}, f32[16]{0:T(128)}, f32[16]{0:T(128)}, f32[16,64]{1,0:T(8,128)}, /*...) custom-call(bf16[2,256,512]{2,1,0:T(8,128)(2,1)} %get-tuple-element., ...), custom_call_target="tpu_custom_call" | custom-call | tf_op jit(solution)/shard_map/pallas_call | solution.py:1176

commit v4 on v3

--- a/solution.py
+++ b/solution.py
@@ -211,7 +211,7 @@
 MESH = pl.DeviceIdType.MESH
 F32, BF16, I16 = (jnp.float32, jnp.bfloat16, jnp.int16)
 STEPS = 32700.0
-GROUP = 4
+GROUP = 8
 HALVES = 2
 
 
@@ -753,9 +753,9 @@
     over_couples(0, lambda p, c: tables_middle(p))
     weight_wait(0)
     weight_hop(1)
+    forward_first(0)
     over_couples(1, lambda p, c: tables_middle(p))
-    for k in range(HALVES):
-        forward_first(k)
+    forward_first(1)
     for k in range(HALVES):
         forward_local(k)
     for k in range(HALVES):

time: 59.8 us -> 59.4 us (level)
  no operation moved by 1% of the time
where the time goes in v4:
time: 59.4 us; the launch traced here: 59.3 us
  Pallas kernels  58.4 us (98%)
  between operations  0.83 us (1%)
    pallas_call x1, Pallas kernels, in_one_kernel(): pl.pallas_call(kernel, out_shape=(jax.ShapeDtypeStruct(inputs.shape, BF16...  56.1 us
    pallas_call x1, Pallas kernels, handed_over(): pl.pallas_call(kernel, out_shape=[jax.ShapeDtypeStruct(shape, value.dtype...  2.33 us

profile of v4, /device:TPU:0, one launch (start us, length us, event | category | flops | bytes accessed | tf_op | source)
XLA Modules:
  0.0 59.3 jit_solution(11837970531477751990)
XLA Ops:
  0.6 56.1 %shard_map.203 = (bf16[2,256,512]{2,1,0:T(8,128)(2,1)}, bf16[2,256,512]{2,1,0:T(8,128)(2,1)}, f32[1,16]{1,0:T(1,128)}, f32[1,16]{1,0:T(1,128)}, f32[16,64]{1,0:T...) custom-call(bf16[2,256,512]{2,1,0:T(8,128)(2,1)} %refs_0_.1, ...), custom_call_target="tpu_custom_call" | custom-call | tf_op jit(solution)/shard_map/pallas_call | solution.py:1197
  56.8 2.3 %shard_map.204 = (bf16[2,256,512]{2,1,0:T(8,128)(2,1)}, bf16[2,256,512]{2,1,0:T(8,128)(2,1)}, f32[16]{0:T(128)}, f32[16]{0:T(128)}, f32[16,64]{1,0:T(8,128)}, /*...) custom-call(bf16[2,256,512]{2,1,0:T(8,128)(2,1)} %get-tuple-element., ...), custom_call_target="tpu_custom_call" | custom-call | tf_op jit(solution)/shard_map/pallas_call | solution.py:1176
